TPU v7x, 1024 devices: a whole 4x4x32 slice. The times are simulated.
1024 devices in a mesh: grp: 64 (over z, core), tp: 16 (over y, x).
Axes of the slice: x: 4, y: 4, z: 32, core: 2. Of those that a mesh axis runs over, the one named last changes fastest.
Arguments:
- hidden: bfloat16 [24576, 5120], P('grp'), may hold values from -6 to 6
- merge_weight: bfloat16 [5120, 8192], P(None, 'tp'), may hold values from -0.078125 to 0.078125
- text_embed: bfloat16 [65536, 8192], P('grp', 'tp'), may hold values from -6 to 6
- gain: float32 [8192], P('tp'), may hold values from 0.1 to 1.9
- head_weight: float32 [8192, 19], P('tp'), may hold values from -2 to 2
- owner: int32 [24576, 1], P('grp'), may hold values from 0 to 63; in each aligned block of 384 rows (0 to 383, 384 to 767, ...) at most 12 rows name the same one
- vis_row: int32 [64, 768], P('grp'), may hold values from 0 to 1023, as said below
- lengths: int32 [64], P('grp'), may hold values from 256 to 1024
- labels: int32 [64, 19], replicated, may hold values from 0 to 1, as said below
- targets: float32 [64, 19], P('grp'), may hold values from -4 to 4
Outputs:
- reward: float32 [64, 19], P('grp')
- visual_grad: bfloat16 [24576, 8192], P('grp', 'tp')
- head_grad: float32 [8192, 19], P('tp')
- gain_grad: float32 [8192], P('tp')
Inputs may be any that keep to these rules, and one draw needn't show every extreme that they name: `owner`: in each vision group's 384 rows no sample is named more than 12 times, a bound that some block reaches. `vis_row`: each row holds 768 different positions. `labels`: an objective may be rated by no sample.
All inputs are finite; a program needn't handle non-finite values.
Results may differ from a plain program's by a relative error of at most 0.0035.
Values may be sent and summed in bfloat16 or wider, within the bound.
No kernel may reach another device: no remote copies, remote signals or barrier semaphores. Data moves between devices by JAX's collectives and lax.ppermute only.
A program may use at most 64 MiB of HBM per device.

v0:
```python
import functools

import jax
import jax.numpy as jnp
from jax import lax
from jax.sharding import Mesh
from jax.sharding import PartitionSpec as P

D = 8192
GRP = ("grp_0", "grp_1")


epsilon = 1e-06


def in_one_piece(arrays, axis, split_dim, concat_dim, along):
    columns = [a.reshape(*a.shape[:along], -1) for a in arrays]
    both = jnp.concatenate(columns, axis=along)
    result, at, gathered = (
        lax.all_to_all(both, axis, split_axis=split_dim, concat_axis=concat_dim, tiled=True),
        0,
        [],
    )
    for a, column in zip(arrays, columns):
        piece = result[..., at : at + column.shape[along]]
        gathered.append(piece.reshape(*piece.shape[:along], *a.shape[along:]))
        at += column.shape[along]
    return tuple(gathered)


def sent_to_all(array, axis):
    copies = jnp.broadcast_to(array, (lax.axis_size(axis), *array.shape))
    return lax.all_to_all(copies, axis, split_axis=0, concat_axis=0, tiled=True)


def over_copies(array, axis):
    everything = sent_to_all(array, axis)
    return jnp.sum(everything, axis=0)


def in_one(arrays, axis):
    ends = [0]
    for a in arrays:
        ends.append(ends[-1] + a.size)
    so_far = over_copies(jnp.concatenate([a.ravel() for a in arrays]), axis)
    return tuple((so_far[b:e].reshape(a.shape) for a, b, e in zip(arrays, ends, ends[1:])))


def one_axis_at_a_time(array, axes):
    return functools.reduce(lax.psum, axes, array)


def on_device(
    hidden, merge_weight, text_embed, gain, head_weight, owner, vis_row, lengths, labels, targets
):
    groups = lax.axis_size(GRP)
    rows_dev = hidden.shape[0]
    capacity = 2 * rows_dev // groups
    width_dev = merge_weight.shape[1]
    positions = text_embed.shape[0]
    objectives = head_weight.shape[1]
    loss_scale = float(positions * groups // 16)
    visual = jnp.dot(hidden, merge_weight, preferred_element_type=jnp.float32).astype(jnp.bfloat16)
    owners = owner[:, 0]
    onehot = (owners[:, None] == jnp.arange(groups, dtype=jnp.int32)[None, :]).astype(jnp.int32)
    slot_rank = jnp.sum(jnp.cumsum(onehot, axis=0) * onehot, axis=1) - 1
    outbox = (
        jnp.zeros((groups, capacity, width_dev), jnp.bfloat16).at[owners, slot_rank].set(visual)
    )
    live_flags = jnp.zeros((groups, capacity), jnp.bfloat16).at[owners, slot_rank].set(1.0)
    arrived, arrived_flags = in_one_piece((outbox, live_flags), GRP, 0, 0, 2)
    arrived = arrived.reshape(groups * capacity, width_dev)
    arrived_flags = arrived_flags.reshape(groups * capacity)
    vis_rows = vis_row[0]
    current = text_embed[vis_rows]
    chosen = jnp.where(arrived_flags[:, None] > 0, arrived, current)
    xfull = text_embed.at[vis_rows].set(chosen).astype(jnp.float32)
    row_sq = jnp.sum(xfull * xfull, axis=1)
    partial_value = jnp.dot(xfull * gain[None, :], head_weight, precision=lax.Precision.HIGHEST)
    length = lengths[0]
    live_rows = (jnp.arange(positions, dtype=jnp.int32) < length).astype(jnp.float32)
    counts = jnp.sum(labels.astype(jnp.float32), axis=0)
    marks = lax.dynamic_index_in_dim(labels, lax.axis_index(GRP), 0, keepdims=False).astype(
        jnp.float32
    )
    target = targets[0]
    total_sq, total_partial = in_one((row_sq, partial_value), "tp")
    inv_rms = lax.rsqrt(total_sq / D + epsilon)
    row_weight = live_rows * inv_rms / length.astype(jnp.float32)
    reward = jnp.sum(row_weight[:, None] * total_partial, axis=0)
    cotangent = loss_scale * marks * (reward - target) / jnp.maximum(counts, 1.0)
    row_dot = jnp.dot(total_partial, cotangent, precision=lax.Precision.HIGHEST)
    head_dir = jnp.dot(head_weight, cotangent, precision=lax.Precision.HIGHEST)
    beta_row = row_weight * inv_rms * inv_rms * row_dot / D
    pooled = jnp.sum(row_weight[:, None] * xfull, axis=0)
    head_grad, gain_grad = (
        one_axis_at_a_time(jnp.outer(gain * pooled, cotangent), GRP),
        one_axis_at_a_time(pooled * head_dir, GRP),
    )
    coefs = jnp.stack([row_weight[vis_rows], beta_row[vis_rows]], axis=-1).reshape(
        groups, capacity, 2
    )
    spread = jnp.broadcast_to(cotangent[None, :], (groups, objectives))
    coef_back, cot_back = in_one_piece((coefs, spread), GRP, 0, 0, 1)
    own_coefs = coef_back[owners, slot_rank]
    own_dirs = jnp.dot(cot_back[owners], head_weight.T, precision=lax.Precision.HIGHEST)
    visual_grad = (
        own_coefs[:, 0:1] * (gain[None, :] * own_dirs)
        - own_coefs[:, 1:2] * visual.astype(jnp.float32)
    ).astype(jnp.bfloat16)
    return (reward[None, :], visual_grad, head_grad, gain_grad)


def solution(mesh):
    torus = Mesh(mesh.devices.reshape(32, 2, mesh.shape["tp"]), ("grp_0", "grp_1", "tp"))
    placed = (
        P(GRP, None),
        P(None, "tp"),
        P(GRP, "tp"),
        P("tp"),
        P("tp", None),
        P(GRP, None),
        P(GRP, None),
        P(GRP),
        P(),
        P(GRP, None),
    )
    return jax.shard_map(
        on_device,
        mesh=torus,
        in_specs=placed,
        out_specs=(P(GRP, None), P(GRP, "tp"), P("tp", None), P("tp")),
        check_vma=False,
    )
```

profile of v0, /device:TPU:1, one launch (start us, length us, event | category | flops | bytes accessed | tf_op | source)
XLA Modules:
  0.0 397.3 jit_solution(15454692828329489131)
XLA Ops:
  0.7 0.7 copy-done.6
  1.4 0.9 reduce-window.6
  2.7 20.7 %scatter_fusion.1 = bf16[64,12]{0,1:T(8,128)(2,1)S(1)} fusion(bf16[64,12]{0,1:T(8,128)(2,1)S(1)} %broadcast_in_dim.21, s32[384]{0:T(512)S(1)} %get-tuple-element.7, bf16[384]{0:T(512)(128)(2,1)S(1)} %broadcast.169), kind=kCustom, calls=%fused_computation.6 | custom fusion | bytes 5376 | tf_op jit(solution)/shard_map/scatter | solution.py:70
  23.6 5.9 %convolution_convert_fusion = bf16[384,512]{1,0:T(8,128)(2,1)S(1)} fusion(bf16[384,5120]{1,0:T(8,128)(2,1)} %param.10, bf16[5120,512]{1,0:T(8,128)(2,1)} %param.11), kind=kOutput, calls=%fused_computation.18 | convolution fusion | flops 2013462528 | bytes 9568256 | tf_op jit(solution)/shard_map/dot_general | solution.py:63
  29.6 21.4 %scatter_fusion = bf16[64,12,512]{2,0,1:T(8,128)(2,1)S(1)} fusion(bf16[64,12,512]{2,0,1:T(8,128)(2,1)S(1)} %broadcast_in_dim.20, s32[384]{0:T(512)S(1)} %get-tuple-element.7, bf16[384,512]{1,0:T(8,128)(2,1)S(1)} %convolution_convert_fusion), kind=kCustom, calls=%fused_computation.5 | custom fusion | bytes 1182720 | tf_op jit(solution)/shard_map/scatter | solution.py:68
  51.1 1.6 copy.44
  52.8 30.4 %all-to-all-start = ((bf16[64,12,513]{2,1,0:T(8,128)(2,1)}), bf16[64,12,513]{2,1,0:T(8,128)(2,1)S(1)}, u32[]{:S(2)}, u32[]{:S(2)}) async-start(bf16[64,12,513]{2,1,0:T(8,128)(2,1)} %copy.44), calls=%async_computation | async-start | bytes 2621440 | tf_op jit(solution)/shard_map/all_to_all | solution.py:20
  83.2 130.3 %all-to-all-done = bf16[64,12,513]{2,1,0:T(8,128)(2,1)S(1)} async-done(((bf16[64,12,513]{2,1,0:T(8,128)(2,1)}), bf16[64,12,513]{2,1,0:T(8,128)(2,1)S(1)}, u32[]{:S(2)}, u32[]{:S(2)}) %all-to-all-start) | async-done | bytes 788000 | tf_op jit(solution)/shard_map/all_to_all | solution.py:20
  213.7 1.1 reshape.123
  214.7 1.2 compare_reduce_fusion
  216.0 12.4 %scatter_custom_fusion.2 = bf16[1024,512]{1,0:T(8,128)(2,1)S(1)} fusion(bf16[1024,512]{1,0:T(8,128)(2,1)S(1)} %copy-done.1, s32[768]{0:T(1024)S(1)} %fusion.17, bf16[768,512]{1,0:T(8,128)(2,1)} %reshape.123, pred[768]{0:T(1024)(128)(4,1)S(1)} %gt.16, s32[1024]{0:T(1024)S(1)} %pad_clamp_fusion.1), kind=kCustom, calls=%fused_computation.21 | custom fusion | flops 393216 | bytes 2888704 | tf_op jit(solution)/shard_map/scatter | solution.py:77
  228.7 1.8 fusion.1
  230.9 2.1 broadcast_in_dim.24
  233.0 6.8 %all-to-all-start.1 = ((f32[16,1,20480]{2,1,0:T(1,128)}), f32[16,1,20480]{2,1,0:T(1,128)S(1)}, u32[]{:S(2)}, u32[]{:S(2)}) async-start(f32[16,1,20480]{2,1,0:T(1,128)} %broadcast_in_dim.24), calls=%async_computation.1 | async-start | bytes 2621440 | tf_op jit(solution)/shard_map/all_to_all | solution.py:33
  240.7 15.8 %all-to-all-done.1 = f32[16,1,20480]{2,1,0:T(1,128)S(1)} async-done(((f32[16,1,20480]{2,1,0:T(1,128)}), f32[16,1,20480]{2,1,0:T(1,128)S(1)}, u32[]{:S(2)}, u32[]{:S(2)}) %all-to-all-start.1) | async-done | bytes 1310752 | tf_op jit(solution)/shard_map/all_to_all | solution.py:33
  256.5 0.9 reduce_sum.56
  258.5 3.2 gather_fusion
  262.3 3.2 gather_fusion.1
  266.5 10.6 %all-to-all-start.2 = ((f32[64,1,43]{2,1,0:T(1,128)}), f32[64,1,43]{2,1,0:T(1,128)S(1)}, u32[]{:S(2)}, u32[]{:S(2)}) async-start(f32[64,1,43]{2,1,0:T(1,128)} %bitcast.10), calls=%async_computation.2 | async-start | bytes 65536 | tf_op jit(solution)/shard_map/all_to_all | solution.py:20
  277.2 82.7 %all-reduce = (f32[512,19]{0,1:T(8,128)S(1)}, f32[512]{0:T(512)S(1)}) all-reduce(f32[512,19]{0,1:T(8,128)S(1)} %broadcast_multiply_fusion, f32[512]{0:T(512)S(1)} %get-tuple-element.13), channel_id=1, replica_groups=mesh['grp_0'=32,'grp_1'=2,'tp'=16] {'grp_0'}, use_global_device_ids=true, to_apply=%region_11.12 | all-reduce | flops 10240 | bytes 81920 | tf_op jit(solution)/shard_map/psum | solution.py:50
  359.9 30.5 %all-reduce.1 = (f32[512,19]{0,1:T(8,128)}, f32[512]{0:T(512)}) all-reduce(f32[512,19]{0,1:T(8,128)S(1)} %get-tuple-element.9, f32[512]{0:T(512)S(1)} %get-tuple-element.10), channel_id=1, replica_groups=mesh['grp_0'=32,'grp_1'=2,'tp'=16] {'grp_1'}, use_global_device_ids=true, to_apply=%region_12.13 | all-reduce | flops 10240 | bytes 81920 | tf_op jit(solution)/shard_map/psum | solution.py:50
  390.7 3.6 gather_fusion.2
  394.6 1.1 gather_fusion.3
  395.7 1.6 fusion.5
  (65 shorter events, 5.5 us)
Async XLA Ops:
  0.6 228.1 %copy-start = (f32[512,19]{0,1:T(8,128)S(1)}, f32[512,19]{0,1:T(8,128)}, u32[]{:S(2)}) copy-start(f32[512,19]{0,1:T(8,128)} %param.14) | copy-start | bytes 116740
  0.6 0.7 copy-start.6
  29.5 21.5 %copy-start.2 = (bf16[384,512]{1,0:T(8,128)(2,1)}, bf16[384,512]{1,0:T(8,128)(2,1)S(1)}, u32[]{:S(2)}) copy-start(bf16[384,512]{1,0:T(8,128)(2,1)S(1)} %convolution_convert_fusion) | copy-start | bytes 1179652
  51.1 32.1 %copy-start.8 = (s32[1,768]{1,0:T(1,128)S(1)}, s32[1,768]{1,0:T(1,128)}, u32[]{:S(2)}) copy-start(s32[1,768]{1,0:T(1,128)} %param.16) | copy-start | bytes 9220
  52.8 160.7 %all-to-all-start = ((bf16[64,12,513]{2,1,0:T(8,128)(2,1)}), bf16[64,12,513]{2,1,0:T(8,128)(2,1)S(1)}, u32[]{:S(2)}, u32[]{:S(2)}) async-start(bf16[64,12,513]{2,1,0:T(8,128)(2,1)} %copy.44), calls=%async_computation | async-start | bytes 2621440 | tf_op jit(solution)/shard_map/all_to_all | solution.py:20
  83.2 132.8 %copy-start.1 = (bf16[1024,512]{1,0:T(8,128)(2,1)S(1)}, bf16[1024,512]{1,0:T(8,128)(2,1)}, u32[]{:S(2)}) copy-start(bf16[1024,512]{1,0:T(8,128)(2,1)} %param.12) | copy-start | bytes 3145732
  214.7 14.0 %copy-start.5 = (f32[512]{0:T(512)S(1)}, f32[512]{0:T(512)}, u32[]{:S(2)}) copy-start(f32[512]{0:T(512)} %param.13) | copy-start | bytes 6148
  230.9 9.6 %copy-start.4 = (s32[64,19]{0,1:T(8,128)S(1)}, s32[64,19]{0,1:T(8,128)}, u32[]{:S(2)}) copy-start(s32[64,19]{0,1:T(8,128)} %param.18) | copy-start | bytes 14596
  233.0 23.5 %all-to-all-start.1 = ((f32[16,1,20480]{2,1,0:T(1,128)}), f32[16,1,20480]{2,1,0:T(1,128)S(1)}, u32[]{:S(2)}, u32[]{:S(2)}) async-start(f32[16,1,20480]{2,1,0:T(1,128)} %broadcast_in_dim.24), calls=%async_computation.1 | async-start | bytes 2621440 | tf_op jit(solution)/shard_map/all_to_all | solution.py:33
  239.7 18.5 %copy-start.9 = (f32[1,19]{1,0:T(1,128)S(1)}, f32[1,19]{1,0:T(1,128)}, u32[]{:S(2)}) copy-start(f32[1,19]{1,0:T(1,128)} %param.19) | copy-start | bytes 232
  258.3 3.4 copy-start.7
  266.5 123.8 %all-to-all-start.2 = ((f32[64,1,43]{2,1,0:T(1,128)}), f32[64,1,43]{2,1,0:T(1,128)S(1)}, u32[]{:S(2)}, u32[]{:S(2)}) async-start(f32[64,1,43]{2,1,0:T(1,128)} %bitcast.10), calls=%async_computation.2 | async-start | bytes 65536 | tf_op jit(solution)/shard_map/all_to_all | solution.py:20
  390.7 5.0 %copy-start.3 = (bf16[384,512]{1,0:T(8,128)(2,1)S(1)}, bf16[384,512]{1,0:T(8,128)(2,1)}, u32[]{:S(2)}) copy-start(bf16[384,512]{1,0:T(8,128)(2,1)} %copy-done.2) | copy-start | bytes 1179652
where the time goes:
time: 398 us; the launch traced here: 397 us
  waiting for transfers between devices  146 us (37%)
  blocking collectives  113 us (28%)
  local copies, waits for them, and re-layouts  61.4 us (15%)
  starting transfers between devices  47.7 us (12%)
  other arithmetic  17.3 us (4%)
  matrix products  9.91 us (2%)
    all_to_all x2, waiting for transfers between devices, in_one_piece(): lax.all_to_all(both, axis, split_axis=split_dim, concat_axis=concat_dim,...  130 us
    psum x2, blocking collectives, one_axis_at_a_time(): return functools.reduce(lax.psum, axes, array)  113 us
    all_to_all x2, starting transfers between devices, in_one_piece(): lax.all_to_all(both, axis, split_axis=split_dim, concat_axis=concat_dim,...  41 us
    scatter x1, local copies, waits for them, and re-layouts, on_device(): jnp.zeros((groups, capacity, width_dev), jnp.bfloat16).at[owners, slot_rank]  21.4 us
    scatter x1, local copies, waits for them, and re-layouts, on_device(): jnp.zeros((groups, capacity), jnp.bfloat16).at[owners, slot_rank].set(1.0)  20.7 us
    all_to_all x1, waiting for transfers between devices, sent_to_all(): return lax.all_to_all(copies, axis, split_axis=0, concat_axis=0, tiled=True)  15.8 us
    scatter x1, other arithmetic, on_device(): xfull = text_embed.at[vis_rows].set(chosen).astype(jnp.float32)  12.4 us
  transfers between devices with their start and end apart: 3, of which 2 were waited for; matrix products, arithmetic and copies ran while one was open for 0% of the time, Pallas kernels for 0%

commit v1 on v0

v1 whole, which is shorter than its diff:
```python
import functools

import jax
import jax.numpy as jnp
from jax import lax
from jax.experimental import pallas as pl
from jax.experimental.pallas import tpu as pltpu
from jax.sharding import Mesh
from jax.sharding import PartitionSpec as P

GRP = ("far", "near", "core")
NEAR = ("near", "core")
TP = ("ty", "tx")
EPSILON = 1e-06
LANES = 128
K_ROWS = 24
TARGET_AT = 32
VMEM = pltpu.CompilerParams(vmem_limit_bytes=48 * 2**20)
EXACT = lax.Precision.HIGHEST
LAST = (((1,), (1,)), ((), ()))
FIRST = (((0,), (0,)), ((), ()))


def iota(shape, dim):
    return lax.broadcasted_iota(jnp.int32, shape, dim)


def in_three(x):
    hi = x.astype(jnp.bfloat16)
    rest = x - hi.astype(jnp.float32)
    mid = rest.astype(jnp.bfloat16)
    return hi, mid, (rest - mid.astype(jnp.float32)).astype(jnp.bfloat16)


def dot32(a, b, dims):
    return lax.dot_general(a, b, dims, preferred_element_type=jnp.float32)


def dot_exact(a, b, dims):
    return lax.dot_general(a, b, dims, precision=EXACT, preferred_element_type=jnp.float32)


def flags_kernel(cap, length_ref, owner_ref, rows_ref, out_ref):
    groups = out_ref.shape[0]
    slots = rows_ref.shape[1]
    length = length_ref[0]
    live = (rows_ref[...] < length).astype(jnp.float32)
    slot = iota((groups, slots), 1)
    first = iota((groups, slots), 0) * cap
    mine = jnp.where((slot >= first) & (slot < first + cap), live, 0.0).astype(jnp.bfloat16)
    rank = lax.rem(iota((LANES, slots), 1), cap)
    place = (rank == iota((LANES, slots), 0)).astype(jnp.bfloat16)
    flags = dot32(mine, place, LAST)
    owned = (owner_ref[...] == iota((groups, owner_ref.shape[1]), 0)).astype(jnp.float32)
    count = jnp.sum(owned, axis=1, keepdims=True)
    lane = iota((groups, LANES), 1)
    flags = jnp.where(lane == cap, count, flags)
    out_ref[...] = jnp.where(lane == cap + 1, length.astype(jnp.float32), flags)


def stats_kernel(
    objectives, hidden_ref, weight_ref, text_ref, gain_ref, head_ref, visual_ref, stats_ref, total, stats
):
    step = pl.program_id(0)
    tokens = total.shape[0]
    gained = jnp.concatenate(in_three(gain_ref[...] * head_ref[...]), axis=0)

    def of_rows(x):
        parts = dot32(gained, x, LAST)
        value = parts[:K_ROWS] + parts[K_ROWS : 2 * K_ROWS] + parts[2 * K_ROWS :]
        wide = x.astype(jnp.float32)
        square = wide * wide
        high = square.astype(jnp.bfloat16)
        low = (square - high.astype(jnp.float32)).astype(jnp.bfloat16)
        ones = jnp.ones((K_ROWS, x.shape[1]), jnp.bfloat16)
        squares = dot32(ones, high, LAST) + dot32(ones, low, LAST)
        return jnp.where(iota(value.shape, 0) == objectives, squares, value)

    part = dot32(hidden_ref[...], weight_ref[...], (((1,), (0,)), ((), ())))

    @pl.when(step == 0)
    def _():
        total[...] = part

    @pl.when(step > 0)
    def _():
        total[...] += part

    rows = text_ref.shape[0]
    stats[:, pl.ds(pl.multiple_of(tokens + step * rows, LANES), rows)] = of_rows(text_ref[...])

    @pl.when(step == pl.num_programs(0) - 1)
    def _():
        visual = total[...].astype(jnp.bfloat16)
        visual_ref[...] = visual
        stats[:, :tokens] = of_rows(visual)
        for copy in range(stats_ref.shape[0]):
            stats_ref[copy] = stats[...]


def pooled_kernel(
    cap,
    objectives,
    features,
    me_ref,
    length_ref,
    stats_ref,
    flags_ref,
    owner_ref,
    rows_ref,
    targets_ref,
    visual_ref,
    text_ref,
    pooled_ref,
    kept_ref,
):
    tokens, width = visual_ref.shape
    positions = text_ref.shape[0]
    groups = flags_ref.shape[0]
    slots = rows_ref.shape[1]
    stats = stats_ref[0]
    for part in range(1, stats_ref.shape[0]):
        stats = stats + stats_ref[part]
    inv = lax.rsqrt(stats[objectives : objectives + 1] / features + EPSILON)
    flags = flags_ref[...]

    owned = owner_ref[...] == iota((groups, tokens), 0)
    member = owned.astype(jnp.bfloat16)
    before = (iota((tokens, tokens), 0) < iota((tokens, tokens), 1)).astype(jnp.bfloat16)
    earlier = dot32(member, before, (((1,), (0,)), ((), ())))
    rank = jnp.sum(jnp.where(owned, earlier, 0.0), axis=0, keepdims=True)
    told = dot_exact(flags, owned.astype(jnp.float32), FIRST)
    at = iota(told.shape, 0)
    live = jnp.sum(
        jnp.where((at < cap) & (at == rank.astype(jnp.int32)), told, 0.0), axis=0, keepdims=True
    )
    token_inv = inv[:, :tokens]
    token_weight = live * token_inv / told[cap + 1 : cap + 2]

    length = length_ref[0]
    slot = iota((groups, slots), 1)
    first = iota((groups, slots), 0) * cap
    count = flags[:, cap : cap + 1].astype(jnp.int32)
    used = jnp.sum(((slot >= first) & (slot < first + count)).astype(jnp.float32), axis=0, keepdims=True)
    row = rows_ref[...]
    tall = positions // LANES
    high = jnp.where(lax.div(row, LANES) == iota((tall, slots), 0), used, 0.0).astype(jnp.bfloat16)
    low = (lax.rem(row, LANES) == iota((LANES, slots), 0)).astype(jnp.bfloat16)
    replaced = dot32(high, low, LAST)
    replaced = jnp.concatenate([replaced[i : i + 1] for i in range(tall)], axis=1)
    stays = (iota((1, positions), 1) < length) & (replaced < 0.5)
    text_weight = jnp.where(stays, inv[:, tokens:], 0.0) / length.astype(jnp.float32)

    along = (((1,), (0,)), ((), ()))
    spread = jnp.where(owned, token_weight, 0.0)
    three = dot32(jnp.concatenate(in_three(spread), axis=0), visual_ref[...], along)
    pooled = three[:groups] + three[groups : 2 * groups] + three[2 * groups :]
    reward = dot_exact(spread, stats[:, :tokens], LAST)
    split = jnp.concatenate(in_three(jnp.broadcast_to(text_weight, (16, positions))), axis=0)
    text_three = dot32(split, text_ref[...], along)
    text_pooled = text_three[0:1] + text_three[16:17] + text_three[32:33]
    text_reward = dot_exact(
        jnp.broadcast_to(text_weight, (8, positions)), stats[:, tokens:], LAST
    )[0:1]
    mine = iota((groups, 1), 0) == me_ref[0]
    pooled_ref[:, :width] = pooled + jnp.where(mine, text_pooled, 0.0)
    reward = reward + jnp.where(mine, text_reward, 0.0)
    target = jnp.where(mine, targets_ref[...], 0.0)
    pooled_ref[:, width:] = jnp.zeros((groups, LANES), jnp.float32)
    pooled_ref[:, width : width + objectives] = reward[:, :objectives]
    pooled_ref[:, width + TARGET_AT : width + TARGET_AT + objectives] = target
    kept = jnp.where(iota((K_ROWS, tokens), 0) == objectives, token_weight, stats[:, :tokens])
    factor = token_weight * token_inv * token_inv / features
    kept_ref[...] = jnp.where(iota((K_ROWS, tokens), 0) == objectives + 1, factor, kept)


def grads_kernel(
    objectives,
    scale,
    me_ref,
    pooled_ref,
    kept_ref,
    owner_ref,
    visual_ref,
    labels_ref,
    gain_ref,
    head_ref,
    reward_ref,
    visual_grad_ref,
    head_grad_ref,
    gain_grad_ref,
):
    tokens, width = visual_ref.shape
    groups = pooled_ref.shape[0]
    z = pooled_ref[:, :width]
    rest = pooled_ref[:, width:]
    mine = iota(rest.shape, 0) == me_ref[0]
    reward_ref[...] = jnp.sum(jnp.where(mine, rest, 0.0), axis=0, keepdims=True)
    turned = rest.T
    labels = labels_ref[...].astype(jnp.float32)
    count = jnp.maximum(jnp.sum(labels, axis=1, keepdims=True), 1.0)
    error = turned[:K_ROWS] - turned[TARGET_AT : TARGET_AT + K_ROWS]
    cot = scale * labels * error / count
    gain = gain_ref[...]
    head = head_ref[...]
    along = (((1,), (0,)), ((), ()))
    head_grad_ref[...] = (gain * dot_exact(cot, z, along))[:objectives]
    direction = dot_exact(cot, head, FIRST)
    gain_grad_ref[...] = jnp.sum(z * direction, axis=0, keepdims=True)
    owned = owner_ref[...] == iota((groups, tokens), 0)
    kept = kept_ref[...]
    own_cot = dot_exact(cot, owned.astype(jnp.float32), along)
    is_value = iota(kept.shape, 0) < objectives
    row_dot = jnp.sum(jnp.where(is_value, kept * own_cot, 0.0), axis=0, keepdims=True)
    weight = kept[objectives : objectives + 1]
    beta = kept[objectives + 1 : objectives + 2] * row_dot
    both = jnp.concatenate([weight, beta, jnp.zeros((LANES - 2, tokens), jnp.float32)], axis=0)
    columns = both.T
    member = owned.astype(jnp.bfloat16)
    directions = jnp.concatenate(in_three(gain * direction), axis=0)
    own = dot32(jnp.concatenate([member] * 3, axis=0), directions, FIRST)
    grad = columns[:, 0:1] * own - columns[:, 1:2] * visual_ref[...].astype(jnp.float32)
    visual_grad_ref[...] = grad.astype(jnp.bfloat16)


def whole(count):
    return [pl.BlockSpec(memory_space=pltpu.VMEM)] * count


def scalars(count):
    return [pl.BlockSpec(memory_space=pltpu.SMEM)] * count


def to_all(array, axis):
    copies = jnp.broadcast_to(array, (lax.axis_size(axis), *array.shape))
    return lax.all_to_all(copies, axis, split_axis=0, concat_axis=0, tiled=True)


def on_device(
    hidden, merge_weight, text_embed, gain, head_weight, owner, vis_row, lengths, labels, targets
):
    groups, near = lax.axis_size(GRP), lax.axis_size(NEAR)
    tokens, depth = hidden.shape
    positions, width = text_embed.shape
    objectives = head_weight.shape[1]
    cap = vis_row.shape[1] // groups
    features = float(width * lax.axis_size(TP))
    scale = float(positions * groups // 16)
    me = lax.axis_index(GRP).astype(jnp.int32).reshape(1)
    owners = owner.reshape(1, tokens)
    gain_row = gain.reshape(1, width)
    head = jnp.pad(head_weight.T, ((0, K_ROWS - objectives), (0, 0)))
    marks = jnp.pad(labels.T, ((0, K_ROWS - objectives), (0, 0)))

    flags = pl.pallas_call(
        functools.partial(flags_kernel, cap),
        out_shape=jax.ShapeDtypeStruct((groups, LANES), jnp.float32),
        in_specs=scalars(1) + whole(2),
        out_specs=pl.BlockSpec(memory_space=pltpu.VMEM),
        compiler_params=VMEM,
        name="flags",
    )(lengths, owners, vis_row)
    told = lax.all_to_all(
        flags.reshape(groups, 1, LANES), GRP, split_axis=0, concat_axis=0, tiled=True
    ).reshape(groups, LANES)

    steps = 8
    rows = tokens + positions
    copies = lax.axis_size("tx")
    visual, stats = pl.pallas_call(
        functools.partial(stats_kernel, objectives),
        grid=(steps,),
        out_shape=(
            jax.ShapeDtypeStruct((tokens, width), jnp.bfloat16),
            jax.ShapeDtypeStruct((copies, K_ROWS, rows), jnp.float32),
        ),
        in_specs=[
            pl.BlockSpec((tokens, depth // steps), lambda i: (0, i)),
            pl.BlockSpec((depth // steps, width), lambda i: (i, 0)),
            pl.BlockSpec((positions // steps, width), lambda i: (i, 0)),
            pl.BlockSpec((1, width), lambda i: (0, 0)),
            pl.BlockSpec((K_ROWS, width), lambda i: (0, 0)),
        ],
        out_specs=(
            pl.BlockSpec((tokens, width), lambda i: (0, 0)),
            pl.BlockSpec((copies, K_ROWS, rows), lambda i: (0, 0, 0)),
        ),
        scratch_shapes=[
            pltpu.VMEM((tokens, width), jnp.float32),
            pltpu.VMEM((K_ROWS, rows), jnp.float32),
        ],
        compiler_params=VMEM,
        name="stats",
    )(hidden, merge_weight, text_embed, gain_row, head)
    stats = lax.all_to_all(stats, "tx", split_axis=0, concat_axis=0, tiled=True)
    stats = to_all(jnp.sum(stats, axis=0), "ty")

    pooled, kept = pl.pallas_call(
        functools.partial(pooled_kernel, cap, objectives, features),
        out_shape=(
            jax.ShapeDtypeStruct((groups, width + LANES), jnp.float32),
            jax.ShapeDtypeStruct((K_ROWS, tokens), jnp.float32),
        ),
        in_specs=scalars(2) + whole(7),
        out_specs=tuple(whole(2)),
        compiler_params=VMEM,
        name="pooled",
    )(me, lengths, stats, told, owners, vis_row, targets, visual, text_embed)
    block = pooled.reshape(near, groups // near, width + LANES)
    block = jnp.sum(lax.all_to_all(block, NEAR, split_axis=0, concat_axis=0, tiled=True), axis=0)
    block = jnp.sum(to_all(block, "far"), axis=0)
    pooled = to_all(block, NEAR).reshape(groups, width + LANES)

    reward, visual_grad, head_grad, gain_grad = pl.pallas_call(
        functools.partial(grads_kernel, objectives, scale),
        out_shape=(
            jax.ShapeDtypeStruct((1, LANES), jnp.float32),
            jax.ShapeDtypeStruct((tokens, width), jnp.bfloat16),
            jax.ShapeDtypeStruct((objectives, width), jnp.float32),
            jax.ShapeDtypeStruct((1, width), jnp.float32),
        ),
        in_specs=scalars(1) + whole(7),
        out_specs=tuple(whole(4)),
        compiler_params=VMEM,
        name="grads",
    )(me, pooled, kept, owners, visual, marks, gain_row, head)
    return reward[:, :objectives], visual_grad, head_grad.T, gain_grad.reshape(width)


def solution(mesh):
    groups, tp = mesh.shape["grp"], mesh.shape["tp"]
    near = 4 if groups % 16 == 0 else 2
    ty = 4 if tp % 16 == 0 else 1
    torus = Mesh(
        mesh.devices.reshape(groups // (2 * near), near, 2, ty, tp // ty),
        ("far", "near", "core", "ty", "tx"),
    )
    placed = (
        P(GRP, None),
        P(None, TP),
        P(GRP, TP),
        P(TP),
        P(TP, None),
        P(GRP, None),
        P(GRP, None),
        P(GRP),
        P(),
        P(GRP, None),
    )
    return jax.shard_map(
        on_device,
        mesh=torus,
        in_specs=placed,
        out_specs=(P(GRP, None), P(GRP, TP), P(TP, None), P(TP)),
        check_vma=False,
    )
```

time: 398 us -> 157 us (0.39)
  waiting for transfers between devices: 146 us -> 41.3 us
  blocking collectives: 113 us -> 42.1 us
  local copies, waits for them, and re-layouts: 61.4 us -> 6.38 us
  other arithmetic: 17.3 us -> 0.06 us
  Pallas kernels: 0 us -> 13.4 us
  matrix products: 9.91 us -> 0 us
    psum x2 -> x0, blocking collectives: 113 us -> none  [one_axis_at_a_time(): return functools.reduce(lax.psum, axes, array)]
    all_to_all x3 -> x4, waiting for transfers between devices: 146 us -> 41.3 us  [the longest x1 22.3 us: on_device(): lax.all_to_all(flags.reshape(groups, 1, LANES), GRP, split_axis=0, concat...]
    scatter x2 -> x0, local copies, waits for them, and re-layouts: 42.1 us -> none  [the longest x1 21.4 us: on_device(): jnp.zeros((groups, capacity, width_dev), jnp.bfloat16).at[owners, slot_rank]]
    all_to_all x0 -> x2, blocking collectives: none -> 42.1 us  [the longest x1 30.6 us: to_all(): return lax.all_to_all(copies, axis, split_axis=0, concat_axis=0, tiled=True)]
    pallas_call x0 -> x4, Pallas kernels: none -> 13.4 us  [the longest x1 10 us: on_device(): pl.pallas_call(functools.partial(stats_kernel, objectives), grid=(steps,)...]
    scatter x1 -> x0, other arithmetic: 12.4 us -> none  [on_device(): xfull = text_embed.at[vis_rows].set(chosen).astype(jnp.float32)]
    gather x4 -> x0, local copies, waits for them, and re-layouts: 11.1 us -> none  [the longest x1 3.6 us: on_device(): own_coefs = coef_back[owners, slot_rank]]
    dot_general x5 -> x0, matrix products: 9.91 us -> none  [the longest x1 5.88 us: on_device(): jnp.dot(hidden, merge_weight, preferred_element_type=jnp.float32)]
  transfers between devices with their start and end apart: 3 -> 4, of which waited for: 2 -> 4; matrix products, arithmetic and copies ran while one was open for 0% -> 0% of each run, Pallas kernels for 0% -> 1%
where the time goes in v1:
time: 157 us; the launch traced here: 156 us
  starting transfers between devices  51.6 us (33%)
  blocking collectives  42.1 us (27%)
  waiting for transfers between devices  41.3 us (26%)
  Pallas kernels  13.4 us (9%)
  local copies, waits for them, and re-layouts  6.38 us (4%)
    all_to_all x1, starting transfers between devices, on_device(): lax.all_to_all(flags.reshape(groups, 1, LANES), GRP, split_axis=0, concat...  32.5 us
    all_to_all x1, blocking collectives, to_all(): return lax.all_to_all(copies, axis, split_axis=0, concat_axis=0, tiled=True)  30.6 us
    all_to_all x1, waiting for transfers between devices, on_device(): lax.all_to_all(flags.reshape(groups, 1, LANES), GRP, split_axis=0, concat...  22.3 us
    all_to_all x2, starting transfers between devices, to_all(): return lax.all_to_all(copies, axis, split_axis=0, concat_axis=0, tiled=True)  14.1 us
    all_to_all x2, waiting for transfers between devices, to_all(): return lax.all_to_all(copies, axis, split_axis=0, concat_axis=0, tiled=True)  13.5 us
    all_to_all x1, blocking collectives, on_device(): lax.all_to_all(block, NEAR, split_axis=0, concat_axis=0, tiled=True)  11.5 us
    pallas_call x1, Pallas kernels, on_device(): pl.pallas_call(functools.partial(stats_kernel, objectives), grid=(steps,)...  10 us
    all_to_all x1, waiting for transfers between devices, on_device(): stats = lax.all_to_all(stats, 'tx', split_axis=0, concat_axis=0, tiled=True)  5.5 us
  transfers between devices with their start and end apart: 4, of which 4 were waited for; matrix products, arithmetic and copies ran while one was open for 0% of the time, Pallas kernels for 1%

profile of v1, /device:TPU:1, one launch (start us, length us, event | category | flops | bytes accessed | tf_op | source)
XLA Modules:
  0.0 156.2 jit_solution(5531534073019683271)
XLA Ops:
  0.6 0.8 pad.8.head_ref
  1.4 1.2 copy-done
  2.7 2.1 %copy-done.2 = bf16[384,5120]{1,0:T(8,128)(2,1)S(1)} copy-done((bf16[384,5120]{1,0:T(8,128)(2,1)S(1)}, bf16[384,5120]{1,0:T(8,128)(2,1)}, u32[]{:S(2)}) %copy-start.2) | copy-done | bytes 3932184
  4.8 0.7 copy-done.5
  5.5 10.0 %stats.1 = (bf16[384,512]{1,0:T(8,128)(2,1)S(1)}, f32[4,24,1408]{2,1,0:T(8,128)}) custom-call(bf16[384,5120]{1,0:T(8,128)(2,1)S(1)} %copy-done.2, bf16[5120,512]{1,0:T(8,128)(2,1)} %weight_ref.1, bf16[1024,512]{1,0:T(8,128)(2,1)S(1)} %copy-done, f32[1,512]{1,0:T(1,128)S(1)} %bitcast.20, f32[24,512]{1,0:T(8,128)S(1)} %pad.8.head_ref), custom_call_target="tpu_custom_call" | custom-call | tf_op jit(solution)/shard_map/stats/pallas_call | solution.py:270
  15.5 5.0 %all-to-all-start = ((f32[4,24,1408]{2,1,0:T(8,128)}), f32[4,24,1408]{2,1,0:T(8,128)S(1)}, u32[]{:S(2)}, u32[]{:S(2)}) async-start(f32[4,24,1408]{2,1,0:T(8,128)} %get-tuple-element.12), calls=%async_computation | async-start | bytes 1081344 | tf_op jit(solution)/shard_map/all_to_all | solution.py:295
  21.1 0.0 copy-done.3
  21.1 0.0 copy-done.4
  21.1 0.8 flags.1
  22.0 5.5 %all-to-all-done = f32[4,24,1408]{2,1,0:T(8,128)S(1)} async-done(((f32[4,24,1408]{2,1,0:T(8,128)}), f32[4,24,1408]{2,1,0:T(8,128)S(1)}, u32[]{:S(2)}, u32[]{:S(2)}) %all-to-all-start) | async-done | bytes 540704 | tf_op jit(solution)/shard_map/all_to_all | solution.py:295
  27.5 32.5 %all-to-all-start.2 = ((f32[64,1,128]{2,1,0:T(1,128)}), f32[64,1,128]{2,1,0:T(1,128)S(1)}, u32[]{:S(2)}, u32[]{:S(2)}) async-start(f32[64,1,128]{2,1,0:T(1,128)} %bitcast.5), calls=%async_computation.2 | async-start | bytes 65536 | tf_op jit(solution)/shard_map/all_to_all | solution.py:263
  60.0 22.3 %all-to-all-done.2 = f32[64,1,128]{2,1,0:T(1,128)S(1)} async-done(((f32[64,1,128]{2,1,0:T(1,128)}), f32[64,1,128]{2,1,0:T(1,128)S(1)}, u32[]{:S(2)}, u32[]{:S(2)}) %all-to-all-start.2) | async-done | bytes 32800 | tf_op jit(solution)/shard_map/all_to_all | solution.py:263
  82.3 0.8 broadcast_in_dim.9
  83.2 4.2 %all-to-all-start.1 = ((f32[4,24,1408]{2,1,0:T(8,128)}), f32[4,24,1408]{2,1,0:T(8,128)S(1)}, u32[]{:S(2)}, u32[]{:S(2)}) async-start(f32[4,24,1408]{2,1,0:T(8,128)} %broadcast_in_dim.9), calls=%async_computation.1 | async-start | bytes 1081344 | tf_op jit(solution)/shard_map/all_to_all | solution.py:236
  87.4 7.5 %all-to-all-done.1.stats_ref = f32[4,24,1408]{2,1,0:T(8,128)S(1)} async-done(((f32[4,24,1408]{2,1,0:T(8,128)}), f32[4,24,1408]{2,1,0:T(8,128)S(1)}, u32[]{:S(2)}, u32[]{:S(2)}) %all-to-all-start.1) | async-done | bytes 540704 | tf_op jit(solution)/shard_map/all_to_all | solution.py:236
  94.9 0.0 copy-done.7
  94.9 1.0 pooled.1
  95.8 11.5 %all_to_all.30 = f32[8,8,640]{2,1,0:T(8,128)S(1)} all-to-all(f32[8,8,640]{2,1,0:T(8,128)S(1)} %bitcast.15), channel_id=1, replica_groups=mesh['far'=8,'near'=4,'core'=2,'ty'=4,'tx'=4] {'near','core'}, dimensions={0} | all-to-all | bytes 327680 | tf_op jit(solution)/shard_map/all_to_all | solution.py:310
  107.4 30.6 %all_to_all.31 = f32[8,8,640]{2,1,0:T(8,128)S(1)} all-to-all(f32[8,8,640]{2,1,0:T(8,128)S(1)} %broadcast_in_dim.10), channel_id=1, replica_groups=mesh['far'=8,'near'=4,'core'=2,'ty'=4,'tx'=4] {'far'}, dimensions={0} | all-to-all | bytes 327680 | tf_op jit(solution)/shard_map/all_to_all | solution.py:236
  138.0 0.7 broadcast_in_dim.11
  138.7 10.0 %all-to-all-start.5 = ((f32[8,8,640]{2,1,0:T(8,128)}), f32[8,8,640]{2,1,0:T(8,128)S(1)}, u32[]{:S(2)}, u32[]{:S(2)}) async-start(f32[8,8,640]{2,1,0:T(8,128)} %broadcast_in_dim.11), calls=%async_computation.5 | async-start | bytes 327680 | tf_op jit(solution)/shard_map/all_to_all | solution.py:236
  148.6 6.0 %all-to-all-done.5 = f32[8,8,640]{2,1,0:T(8,128)S(1)} async-done(((f32[8,8,640]{2,1,0:T(8,128)}), f32[8,8,640]{2,1,0:T(8,128)S(1)}, u32[]{:S(2)}, u32[]{:S(2)}) %all-to-all-start.5) | async-done | bytes 163872 | tf_op jit(solution)/shard_map/all_to_all | solution.py:236
  154.6 0.0 copy-done.6
  154.6 1.6 %grads.1 = (f32[1,128]{1,0:T(1,128)}, bf16[384,512]{1,0:T(8,128)(2,1)}, f32[19,512]{1,0:T(8,128)}, f32[1,512]{1,0:T(1,128)}) custom-call(s32[1]{0:T(128)} %bitcast.me_ref, f32[64,640]{1,0:T(8,128)S(1)} %bitcast.14, f32[24,384]{1,0:T(8,128)S(1)} %get-tuple-element.15.kept_ref, s32[1,384]{1,0:T(1,128)S(1)} %bitcast.19, ...), custom_call_target="tpu_custom_call" | custom-call | tf_op jit(solution)/shard_map/grads/pallas_call | solution.py:314
  (16 shorter events, 0.1 us)
Async XLA Ops:
  1.4 1.2 copy-start
  2.7 2.1 %copy-start.2 = (bf16[384,5120]{1,0:T(8,128)(2,1)S(1)}, bf16[384,5120]{1,0:T(8,128)(2,1)}, u32[]{:S(2)}) copy-start(bf16[384,5120]{1,0:T(8,128)(2,1)} %hidden_ref.1) | copy-start | bytes 11796484
  4.8 0.7 copy-start.5
  5.5 15.7 %copy-start.3 = (s32[384,1]{0,1:T(1,128)S(1)}, s32[384,1]{0,1:T(1,128)}, u32[]{:S(2)}) copy-start(s32[384,1]{0,1:T(1,128)} %param.15) | copy-start | bytes 4612
  5.5 15.7 %copy-start.4 = (s32[1,768]{1,0:T(1,128)S(1)}, s32[1,768]{1,0:T(1,128)}, u32[]{:S(2)}) copy-start(s32[1,768]{1,0:T(1,128)} %rows_ref.3) | copy-start | bytes 9220
  5.5 89.4 %copy-start.1 = (bf16[1024,512]{1,0:T(8,128)(2,1)S(1)}, bf16[1024,512]{1,0:T(8,128)(2,1)}, u32[]{:S(2)}) copy-start(bf16[1024,512]{1,0:T(8,128)(2,1)} %text_ref.3) | copy-start | bytes 3145732
  5.5 89.4 %copy-start.7 = (f32[1,19]{1,0:T(1,128)S(1)}, f32[1,19]{1,0:T(1,128)}, u32[]{:S(2)}) copy-start(f32[1,19]{1,0:T(1,128)} %targets_ref.1) | copy-start | bytes 232
  15.5 133.1 %copy-start.8 = (s32[64,19]{0,1:T(8,128)S(1)}, s32[64,19]{0,1:T(8,128)}, u32[]{:S(2)}) copy-start(s32[64,19]{0,1:T(8,128)} %param.18) | copy-start | bytes 14596
  15.5 139.1 %copy-start.6 = (f32[512]{0:T(512)S(1)}, f32[512]{0:T(512)}, u32[]{:S(2)}) copy-start(f32[512]{0:T(512)} %param.13) | copy-start | bytes 6148
  15.5 12.0 %all-to-all-start = ((f32[4,24,1408]{2,1,0:T(8,128)}), f32[4,24,1408]{2,1,0:T(8,128)S(1)}, u32[]{:S(2)}, u32[]{:S(2)}) async-start(f32[4,24,1408]{2,1,0:T(8,128)} %get-tuple-element.12), calls=%async_computation | async-start | bytes 1081344 | tf_op jit(solution)/shard_map/all_to_all | solution.py:295
  27.5 54.8 %all-to-all-start.2 = ((f32[64,1,128]{2,1,0:T(1,128)}), f32[64,1,128]{2,1,0:T(1,128)S(1)}, u32[]{:S(2)}, u32[]{:S(2)}) async-start(f32[64,1,128]{2,1,0:T(1,128)} %bitcast.5), calls=%async_computation.2 | async-start | bytes 65536 | tf_op jit(solution)/shard_map/all_to_all | solution.py:263
  83.2 11.7 %all-to-all-start.1 = ((f32[4,24,1408]{2,1,0:T(8,128)}), f32[4,24,1408]{2,1,0:T(8,128)S(1)}, u32[]{:S(2)}, u32[]{:S(2)}) async-start(f32[4,24,1408]{2,1,0:T(8,128)} %broadcast_in_dim.9), calls=%async_computation.1 | async-start | bytes 1081344 | tf_op jit(solution)/shard_map/all_to_all | solution.py:236
  138.7 15.9 %all-to-all-start.5 = ((f32[8,8,640]{2,1,0:T(8,128)}), f32[8,8,640]{2,1,0:T(8,128)S(1)}, u32[]{:S(2)}, u32[]{:S(2)}) async-start(f32[8,8,640]{2,1,0:T(8,128)} %broadcast_in_dim.11), calls=%async_computation.5 | async-start | bytes 327680 | tf_op jit(solution)/shard_map/all_to_all | solution.py:236

commit v2 on v1

--- a/solution.py
+++ b/solution.py
@@ -59,7 +59,17 @@
 
 
 def stats_kernel(
-    objectives, hidden_ref, weight_ref, text_ref, gain_ref, head_ref, visual_ref, stats_ref, total, stats
+    objectives,
+    after_ref,
+    hidden_ref,
+    weight_ref,
+    text_ref,
+    gain_ref,
+    head_ref,
+    visual_ref,
+    stats_ref,
+    total,
+    stats,
 ):
     step = pl.program_id(0)
     tokens = total.shape[0]
@@ -275,6 +285,7 @@
             jax.ShapeDtypeStruct((copies, K_ROWS, rows), jnp.float32),
         ),
         in_specs=[
+            pl.BlockSpec(memory_space=pl.ANY),
             pl.BlockSpec((tokens, depth // steps), lambda i: (0, i)),
             pl.BlockSpec((depth // steps, width), lambda i: (i, 0)),
             pl.BlockSpec((positions // steps, width), lambda i: (i, 0)),
@@ -291,7 +302,8 @@
         ],
         compiler_params=VMEM,
         name="stats",
-    )(hidden, merge_weight, text_embed, gain_row, head)
+    )(flags, hidden, merge_weight, text_embed, gain_row, head)
+    stats, told = lax.optimization_barrier((stats, told))
     stats = lax.all_to_all(stats, "tx", split_axis=0, concat_axis=0, tiled=True)
     stats = to_all(jnp.sum(stats, axis=0), "ty")
 
@@ -329,7 +341,7 @@
 
 def solution(mesh):
     groups, tp = mesh.shape["grp"], mesh.shape["tp"]
-    near = 4 if groups % 16 == 0 else 2
+    near = 8 if groups % 32 == 0 else 2
     ty = 4 if tp % 16 == 0 else 1
     torus = Mesh(
         mesh.devices.reshape(groups // (2 * near), near, 2, ty, tp // ty),

time: 157 us -> 159 us (1.013)
  blocking collectives: 42.1 us -> 66.3 us
  waiting for transfers between devices: 41.3 us -> 28.8 us
  starting transfers between devices: 51.6 us -> 40.9 us
    all_to_all x1, waiting for transfers between devices: 22.3 us -> 8.28 us  [on_device(): lax.all_to_all(flags.reshape(groups, 1, LANES), GRP, split_axis=0, concat...]
    all_to_all x0 -> x1, blocking collectives: none -> 11.6 us  [on_device(): stats = lax.all_to_all(stats, 'tx', split_axis=0, concat_axis=0, tiled=True)]
    all_to_all x1, blocking collectives: 11.5 us -> 20.3 us  [on_device(): lax.all_to_all(block, NEAR, split_axis=0, concat_axis=0, tiled=True)]
    all_to_all x2, waiting for transfers between devices: 13.5 us -> 20.5 us  [to_all(): return lax.all_to_all(copies, axis, split_axis=0, concat_axis=0, tiled=True)]
    all_to_all x1 -> x0, waiting for transfers between devices: 5.5 us -> none  [on_device(): stats = lax.all_to_all(stats, 'tx', split_axis=0, concat_axis=0, tiled=True)]
    all_to_all x1 -> x0, starting transfers between devices: 4.97 us -> none  [on_device(): stats = lax.all_to_all(stats, 'tx', split_axis=0, concat_axis=0, tiled=True)]
    all_to_all x1, blocking collectives: 30.6 us -> 34.4 us  [to_all(): return lax.all_to_all(copies, axis, split_axis=0, concat_axis=0, tiled=True)]
    all_to_all x2, starting transfers between devices: 14.1 us -> 10.5 us  [to_all(): return lax.all_to_all(copies, axis, split_axis=0, concat_axis=0, tiled=True)]
  transfers between devices with their start and end apart: 4 -> 3, of which waited for: 4 -> 3; matrix products, arithmetic and copies ran while one was open for 0% -> 1% of each run, Pallas kernels for 1% -> 6%
where the time goes in v2:
time: 159 us; the launch traced here: 158 us
  blocking collectives  66.3 us (42%)
  starting transfers between devices  40.9 us (26%)
  waiting for transfers between devices  28.8 us (18%)
  Pallas kernels  12.6 us (8%)
  local copies, waits for them, and re-layouts  7.89 us (5%)
    all_to_all x1, blocking collectives, to_all(): return lax.all_to_all(copies, axis, split_axis=0, concat_axis=0, tiled=True)  34.4 us
    all_to_all x1, starting transfers between devices, on_device(): lax.all_to_all(flags.reshape(groups, 1, LANES), GRP, split_axis=0, concat...  30.4 us
    all_to_all x2, waiting for transfers between devices, to_all(): return lax.all_to_all(copies, axis, split_axis=0, concat_axis=0, tiled=True)  20.5 us
    all_to_all x1, blocking collectives, on_device(): lax.all_to_all(block, NEAR, split_axis=0, concat_axis=0, tiled=True)  20.3 us
    all_to_all x1, blocking collectives, on_device(): stats = lax.all_to_all(stats, 'tx', split_axis=0, concat_axis=0, tiled=True)  11.6 us
    all_to_all x2, starting transfers between devices, to_all(): return lax.all_to_all(copies, axis, split_axis=0, concat_axis=0, tiled=True)  10.5 us
    pallas_call x1, Pallas kernels, on_device(): pl.pallas_call(functools.partial(stats_kernel, objectives), grid=(steps,)...  9.17 us
    all_to_all x1, waiting for transfers between devices, on_device(): lax.all_to_all(flags.reshape(groups, 1, LANES), GRP, split_axis=0, concat...  8.28 us
  transfers between devices with their start and end apart: 3, of which 3 were waited for; matrix products, arithmetic and copies ran while one was open for 1% of the time, Pallas kernels for 6%

profile of v2, /device:TPU:1, one launch (start us, length us, event | category | flops | bytes accessed | tf_op | source)
XLA Modules:
  0.0 157.9 jit_solution(11718137868216587387)
XLA Ops:
  1.3 0.0 copy-start.3
  1.3 0.7 copy-done.3
  2.0 0.7 copy-done.5
  2.6 0.8 flags.1.after_ref
  3.5 30.4 %all-to-all-start = ((f32[64,1,128]{2,1,0:T(1,128)}), f32[64,1,128]{2,1,0:T(1,128)S(1)}, u32[]{:S(2)}, u32[]{:S(2)}) async-start(f32[64,1,128]{2,1,0:T(1,128)} %bitcast.5), calls=%async_computation | async-start | bytes 65536 | tf_op jit(solution)/shard_map/all_to_all | solution.py:273
  33.9 0.8 pad.8.head_ref
  34.7 1.2 copy-done
  35.9 2.1 %copy-done.2 = bf16[384,5120]{1,0:T(8,128)(2,1)S(1)} copy-done((bf16[384,5120]{1,0:T(8,128)(2,1)S(1)}, bf16[384,5120]{1,0:T(8,128)(2,1)}, u32[]{:S(2)}) %copy-start.2) | copy-done | bytes 3932184
  38.0 0.7 copy-done.7
  38.7 9.2 %stats.1 = (bf16[384,512]{1,0:T(8,128)(2,1)S(1)}, f32[4,24,1408]{2,1,0:T(8,128)S(1)}) custom-call(f32[64,128]{1,0:T(8,128)} %flags.1.after_ref, bf16[384,5120]{1,0:T(8,128)(2,1)S(1)} %copy-done.2, bf16[5120,512]{1,0:T(8,128)(2,1)} %weight_ref.1, bf16[1024,512]{1,0:T(8,128)(2,1)S(1)} %copy-done, f32[1,512]{1,0:T(1,128)S(1)} %bitcast.16, ...), custom_call_target="tpu_custom_call" | custom-call | tf_op jit(solution)/shard_map/stats/pallas_call | solution.py:280
  47.9 0.0 copy-start.10
  48.0 8.3 %all-to-all-done = f32[64,1,128]{2,1,0:T(1,128)S(1)} async-done(((f32[64,1,128]{2,1,0:T(1,128)}), f32[64,1,128]{2,1,0:T(1,128)S(1)}, u32[]{:S(2)}, u32[]{:S(2)}) %all-to-all-start) | async-done | bytes 32800 | tf_op jit(solution)/shard_map/all_to_all | solution.py:273
  56.2 11.6 %all_to_all.30 = f32[4,24,1408]{2,1,0:T(8,128)S(1)} all-to-all(f32[4,24,1408]{2,1,0:T(8,128)S(1)} %get-tuple-element.15), channel_id=1, replica_groups=mesh['far'=4,'near'=8,'core'=2,'ty'=4,'tx'=4] {'tx'}, dimensions={0} | all-to-all | bytes 1081344 | tf_op jit(solution)/shard_map/all_to_all | solution.py:307
  67.9 0.8 broadcast_in_dim.9
  68.7 4.2 %all-to-all-start.2 = ((f32[4,24,1408]{2,1,0:T(8,128)}), f32[4,24,1408]{2,1,0:T(8,128)S(1)}, u32[]{:S(2)}, u32[]{:S(2)}) async-start(f32[4,24,1408]{2,1,0:T(8,128)} %broadcast_in_dim.9), calls=%async_computation.2 | async-start | bytes 1081344 | tf_op jit(solution)/shard_map/all_to_all | solution.py:246
  72.9 7.0 %all-to-all-done.2.stats_ref = f32[4,24,1408]{2,1,0:T(8,128)S(1)} async-done(((f32[4,24,1408]{2,1,0:T(8,128)}), f32[4,24,1408]{2,1,0:T(8,128)S(1)}, u32[]{:S(2)}, u32[]{:S(2)}) %all-to-all-start.2) | async-done | bytes 540704 | tf_op jit(solution)/shard_map/all_to_all | solution.py:246
  80.0 1.0 pooled.1
  81.0 20.3 %all_to_all.31 = f32[16,4,640]{2,1,0:T(4,128)S(1)} all-to-all(f32[16,4,640]{2,1,0:T(4,128)S(1)} %reshape.37), channel_id=1, replica_groups=mesh['far'=4,'near'=8,'core'=2,'ty'=4,'tx'=4] {'near','core'}, dimensions={0} | all-to-all | bytes 327680 | tf_op jit(solution)/shard_map/all_to_all | solution.py:322
  101.4 34.4 %all_to_all.32 = f32[4,4,640]{2,1,0:T(4,128)S(1)} all-to-all(f32[4,4,640]{2,1,0:T(4,128)S(1)} %broadcast_in_dim.10), channel_id=1, replica_groups=mesh['far'=4,'near'=8,'core'=2,'ty'=4,'tx'=4] {'far'}, dimensions={0} | all-to-all | bytes 81920 | tf_op jit(solution)/shard_map/all_to_all | solution.py:246
  135.7 0.7 broadcast_in_dim.11
  136.4 6.3 %all-to-all-start.5 = ((f32[16,4,640]{2,1,0:T(4,128)}), f32[16,4,640]{2,1,0:T(4,128)S(1)}, u32[]{:S(2)}, u32[]{:S(2)}) async-start(f32[16,4,640]{2,1,0:T(4,128)} %broadcast_in_dim.11), calls=%async_computation.5 | async-start | bytes 327680 | tf_op jit(solution)/shard_map/all_to_all | solution.py:246
  142.7 13.5 %all-to-all-done.5 = f32[16,4,640]{2,1,0:T(4,128)S(1)} async-done(((f32[16,4,640]{2,1,0:T(4,128)}), f32[16,4,640]{2,1,0:T(4,128)S(1)}, u32[]{:S(2)}, u32[]{:S(2)}) %all-to-all-start.5) | async-done | bytes 163872 | tf_op jit(solution)/shard_map/all_to_all | solution.py:246
  156.2 0.1 reshape.38.pooled_ref
  156.3 1.6 %grads.1 = (f32[1,128]{1,0:T(1,128)}, bf16[384,512]{1,0:T(8,128)(2,1)}, f32[19,512]{1,0:T(8,128)}, f32[1,512]{1,0:T(1,128)}) custom-call(s32[1]{0:T(128)} %bitcast.me_ref, f32[64,640]{1,0:T(8,128)S(1)} %reshape.38.pooled_ref, f32[24,384]{1,0:T(8,128)S(1)} %get-tuple-element.19.kept_ref, s32[1,384]{1,0:T(1,128)S(1)} %bitcast.15, ...), custom_call_target="tpu_custom_call" | custom-call | tf_op jit(solution)/shard_map/grads/pallas_call | solution.py:326
  (21 shorter events, 0.2 us)
Async XLA Ops:
  1.3 0.7 copy-start.3
  2.0 0.7 copy-start.5
  3.5 52.8 %all-to-all-start = ((f32[64,1,128]{2,1,0:T(1,128)}), f32[64,1,128]{2,1,0:T(1,128)S(1)}, u32[]{:S(2)}, u32[]{:S(2)}) async-start(f32[64,1,128]{2,1,0:T(1,128)} %bitcast.5), calls=%async_computation | async-start | bytes 65536 | tf_op jit(solution)/shard_map/all_to_all | solution.py:273
  34.7 1.2 copy-start
  35.9 2.1 %copy-start.2 = (bf16[384,5120]{1,0:T(8,128)(2,1)S(1)}, bf16[384,5120]{1,0:T(8,128)(2,1)}, u32[]{:S(2)}) copy-start(bf16[384,5120]{1,0:T(8,128)(2,1)} %hidden_ref.1) | copy-start | bytes 11796484
  38.0 0.7 copy-start.7
  38.7 41.2 %copy-start.1 = (bf16[1024,512]{1,0:T(8,128)(2,1)S(1)}, bf16[1024,512]{1,0:T(8,128)(2,1)}, u32[]{:S(2)}) copy-start(bf16[1024,512]{1,0:T(8,128)(2,1)} %text_ref.3) | copy-start | bytes 3145732
  38.7 41.2 %copy-start.4 = (s32[384,1]{0,1:T(1,128)S(1)}, s32[384,1]{0,1:T(1,128)}, u32[]{:S(2)}) copy-start(s32[384,1]{0,1:T(1,128)} %param.15) | copy-start | bytes 4612
  38.7 41.2 %copy-start.6 = (s32[1,768]{1,0:T(1,128)S(1)}, s32[1,768]{1,0:T(1,128)}, u32[]{:S(2)}) copy-start(s32[1,768]{1,0:T(1,128)} %rows_ref.3) | copy-start | bytes 9220
  38.7 41.2 %copy-start.9 = (f32[1,19]{1,0:T(1,128)S(1)}, f32[1,19]{1,0:T(1,128)}, u32[]{:S(2)}) copy-start(f32[1,19]{1,0:T(1,128)} %targets_ref.1) | copy-start | bytes 232
  47.9 94.8 %copy-start.10 = (s32[64,19]{0,1:T(8,128)S(1)}, s32[64,19]{0,1:T(8,128)}, u32[]{:S(2)}) copy-start(s32[64,19]{0,1:T(8,128)} %param.18) | copy-start | bytes 14596
  48.0 108.3 %copy-start.8 = (f32[512]{0:T(512)S(1)}, f32[512]{0:T(512)}, u32[]{:S(2)}) copy-start(f32[512]{0:T(512)} %param.13) | copy-start | bytes 6148
  68.7 11.2 %all-to-all-start.2 = ((f32[4,24,1408]{2,1,0:T(8,128)}), f32[4,24,1408]{2,1,0:T(8,128)S(1)}, u32[]{:S(2)}, u32[]{:S(2)}) async-start(f32[4,24,1408]{2,1,0:T(8,128)} %broadcast_in_dim.9), calls=%async_computation.2 | async-start | bytes 1081344 | tf_op jit(solution)/shard_map/all_to_all | solution.py:246
  136.4 19.8 %all-to-all-start.5 = ((f32[16,4,640]{2,1,0:T(4,128)}), f32[16,4,640]{2,1,0:T(4,128)S(1)}, u32[]{:S(2)}, u32[]{:S(2)}) async-start(f32[16,4,640]{2,1,0:T(4,128)} %broadcast_in_dim.11), calls=%async_computation.5 | async-start | bytes 327680 | tf_op jit(solution)/shard_map/all_to_all | solution.py:246

commit v3 on v2

--- a/solution.py
+++ b/solution.py
@@ -104,8 +104,7 @@
         visual = total[...].astype(jnp.bfloat16)
         visual_ref[...] = visual
         stats[:, :tokens] = of_rows(visual)
-        for copy in range(stats_ref.shape[0]):
-            stats_ref[copy] = stats[...]
+        stats_ref[...] = stats[...]
 
 
 def pooled_kernel(
@@ -241,11 +240,6 @@
     return [pl.BlockSpec(memory_space=pltpu.SMEM)] * count
 
 
-def to_all(array, axis):
-    copies = jnp.broadcast_to(array, (lax.axis_size(axis), *array.shape))
-    return lax.all_to_all(copies, axis, split_axis=0, concat_axis=0, tiled=True)
-
-
 def on_device(
     hidden, merge_weight, text_embed, gain, head_weight, owner, vis_row, lengths, labels, targets
 ):
@@ -276,13 +270,12 @@
 
     steps = 8
     rows = tokens + positions
-    copies = lax.axis_size("tx")
     visual, stats = pl.pallas_call(
         functools.partial(stats_kernel, objectives),
         grid=(steps,),
         out_shape=(
             jax.ShapeDtypeStruct((tokens, width), jnp.bfloat16),
-            jax.ShapeDtypeStruct((copies, K_ROWS, rows), jnp.float32),
+            jax.ShapeDtypeStruct((K_ROWS, rows), jnp.float32),
         ),
         in_specs=[
             pl.BlockSpec(memory_space=pl.ANY),
@@ -294,7 +287,7 @@
         ],
         out_specs=(
             pl.BlockSpec((tokens, width), lambda i: (0, 0)),
-            pl.BlockSpec((copies, K_ROWS, rows), lambda i: (0, 0, 0)),
+            pl.BlockSpec((K_ROWS, rows), lambda i: (0, 0)),
         ),
         scratch_shapes=[
             pltpu.VMEM((tokens, width), jnp.float32),
@@ -303,9 +296,7 @@
         compiler_params=VMEM,
         name="stats",
     )(flags, hidden, merge_weight, text_embed, gain_row, head)
-    stats, told = lax.optimization_barrier((stats, told))
-    stats = lax.all_to_all(stats, "tx", split_axis=0, concat_axis=0, tiled=True)
-    stats = to_all(jnp.sum(stats, axis=0), "ty")
+    stats = lax.all_gather(jnp.sum(lax.all_gather(stats, "tx"), axis=0), "ty")
 
     pooled, kept = pl.pallas_call(
         functools.partial(pooled_kernel, cap, objectives, features),
@@ -320,8 +311,8 @@
     )(me, lengths, stats, told, owners, vis_row, targets, visual, text_embed)
     block = pooled.reshape(near, groups // near, width + LANES)
     block = jnp.sum(lax.all_to_all(block, NEAR, split_axis=0, concat_axis=0, tiled=True), axis=0)
-    block = jnp.sum(to_all(block, "far"), axis=0)
-    pooled = to_all(block, NEAR).reshape(groups, width + LANES)
+    block = jnp.sum(lax.all_gather(block, "far"), axis=0)
+    pooled = lax.all_gather(block, NEAR, tiled=True)
 
     reward, visual_grad, head_grad, gain_grad = pl.pallas_call(
         functools.partial(grads_kernel, objectives, scale),
@@ -341,7 +332,7 @@
 
 def solution(mesh):
     groups, tp = mesh.shape["grp"], mesh.shape["tp"]
-    near = 8 if groups % 32 == 0 else 2
+    near = 4 if groups % 16 == 0 else 2
     ty = 4 if tp % 16 == 0 else 1
     torus = Mesh(
         mesh.devices.reshape(groups // (2 * near), near, 2, ty, tp // ty),

time: 159 us -> 149 us (0.937)
  waiting for transfers between devices: 28.8 us -> 5.98 us
  blocking collectives: 66.3 us -> 81.1 us
  local copies, waits for them, and re-layouts: 7.89 us -> 6.22 us
    all_gather x0 -> x4, blocking collectives: none -> 81.1 us  [the longest x1 37.9 us: on_device(): block = jnp.sum(lax.all_gather(block, 'far'), axis=0)]
    all_to_all x3 -> x0, blocking collectives: 66.3 us -> none  [the longest x1 34.4 us: to_all(): return lax.all_to_all(copies, axis, split_axis=0, concat_axis=0, tiled=True)]
    all_to_all x2 -> x1, waiting for transfers between devices: 20.5 us -> 5.97 us  [on_device(): lax.all_to_all(block, NEAR, split_axis=0, concat_axis=0, tiled=True)]
    all_to_all x1, waiting for transfers between devices: 8.28 us -> 0.01 us  [on_device(): lax.all_to_all(flags.reshape(groups, 1, LANES), GRP, split_axis=0, concat...]
    all_to_all x2 -> x1, starting transfers between devices: 10.5 us -> 10.4 us  [on_device(): lax.all_to_all(block, NEAR, split_axis=0, concat_axis=0, tiled=True)]
  transfers between devices with their start and end apart: 3 -> 2, of which waited for: 3 -> 1; matrix products, arithmetic and copies ran while one was open for 1% -> 1% of each run, Pallas kernels for 6% -> 6%
where the time goes in v3:
time: 149 us
  blocking collectives  81.1 us (54%)
  starting transfers between devices  40.8 us (27%)
  Pallas kernels  13.2 us (9%)
  local copies, waits for them, and re-layouts  6.22 us (4%)
  waiting for transfers between devices  5.98 us (4%)
    all_gather x1, blocking collectives, on_device(): block = jnp.sum(lax.all_gather(block, 'far'), axis=0)  37.9 us
    all_to_all x1, starting transfers between devices, on_device(): lax.all_to_all(flags.reshape(groups, 1, LANES), GRP, split_axis=0, concat...  30.4 us
    all_gather x2, blocking collectives, on_device(): stats = lax.all_gather(jnp.sum(lax.all_gather(stats, 'tx'), axis=0), 'ty')  21.8 us
    all_gather x1, blocking collectives, on_device(): pooled = lax.all_gather(block, NEAR, tiled=True)  21.4 us
    all_to_all x1, starting transfers between devices, on_device(): lax.all_to_all(block, NEAR, split_axis=0, concat_axis=0, tiled=True)  10.4 us
    pallas_call x1, Pallas kernels, on_device(): pl.pallas_call(functools.partial(stats_kernel, objectives), grid=(steps,)...  9.14 us
    all_to_all x1, waiting for transfers between devices, on_device(): lax.all_to_all(block, NEAR, split_axis=0, concat_axis=0, tiled=True)  5.97 us
    unnamed x22, local copies, waits for them, and re-layouts  5.4 us
  transfers between devices with their start and end apart: 2, of which 1 were waited for; matrix products, arithmetic and copies ran while one was open for 1% of the time, Pallas kernels for 6%

profile of v3, /device:TPU:1, one launch (start us, length us, event | category | flops | bytes accessed | tf_op | source)
XLA Modules:
  0.0 148.7 jit_solution(1122465628657175075)
XLA Ops:
  1.3 0.0 copy-start.3
  1.3 0.7 copy-done.3
  2.0 0.7 copy-done.5
  2.6 0.8 flags.1.after_ref
  3.5 30.4 %all-to-all-start = ((f32[64,1,128]{2,1,0:T(1,128)}), f32[64,1,128]{2,1,0:T(1,128)S(1)}, u32[]{:S(2)}, u32[]{:S(2)}) async-start(f32[64,1,128]{2,1,0:T(1,128)} %bitcast.7), calls=%async_computation | async-start | bytes 65536 | tf_op jit(solution)/shard_map/all_to_all | solution.py:267
  33.9 0.8 pad.8.head_ref
  34.7 1.2 copy-done
  35.9 2.1 %copy-done.2 = bf16[384,5120]{1,0:T(8,128)(2,1)S(1)} copy-done((bf16[384,5120]{1,0:T(8,128)(2,1)S(1)}, bf16[384,5120]{1,0:T(8,128)(2,1)}, u32[]{:S(2)}) %copy-start.2) | copy-done | bytes 3932184
  38.0 0.7 copy-done.7
  38.7 0.0 copy-start.10
  38.8 0.0 copy-start.8
  38.8 9.1 %stats.1 = (bf16[384,512]{1,0:T(8,128)(2,1)S(1)}, f32[24,1408]{1,0:T(8,128)S(1)}) custom-call(f32[64,128]{1,0:T(8,128)} %flags.1.after_ref, bf16[384,5120]{1,0:T(8,128)(2,1)S(1)} %copy-done.2, bf16[5120,512]{1,0:T(8,128)(2,1)} %weight_ref.1, bf16[1024,512]{1,0:T(8,128)(2,1)S(1)} %copy-done, f32[1,512]{1,0:T(1,128)S(1)} %bitcast.22, f32[24,512]{1,0:T(8,128)S(1)} %pad.8.head_ref), custom_call_target="tpu_custom_call" | custom-call | tf_op jit(solution)/shard_map/stats/pallas_call | solution.py:273
  47.9 11.2 %all-gather = f32[96,1408]{1,0:T(8,128)S(1)} all-gather(f32[24,1408]{1,0:T(8,128)S(1)} %get-tuple-element.12), channel_id=2, replica_groups=mesh['far'=8,'near'=4,'core'=2,'ty'=4,'tx'=4] {'tx'}, dimensions={0}, use_global_device_ids=true | all-gather | bytes 675840 | tf_op jit(solution)/shard_map/all_gather | solution.py:299
  59.1 10.7 %all-gather.1 = f32[96,1408]{1,0:T(8,128)S(1)} all-gather(f32[24,1408]{1,0:T(8,128)S(1)} %reduce_sum.27), channel_id=3, replica_groups=mesh['far'=8,'near'=4,'core'=2,'ty'=4,'tx'=4] {'ty'}, dimensions={0}, use_global_device_ids=true | all-gather | bytes 675840 | tf_op jit(solution)/shard_map/all_gather | solution.py:299
  69.8 0.0 all-to-all-done
  69.8 0.0 copy-done.1
  69.8 0.0 copy-done.4
  69.8 0.0 copy-done.6
  69.8 1.6 %pooled.1 = (f32[64,640]{1,0:T(8,128)}, f32[24,384]{1,0:T(8,128)S(1)}) custom-call(s32[1]{0:T(128)} %bitcast.me_ref, s32[1]{0:T(128)S(6)} %copy.16.length_ref, f32[4,24,1408]{2,1,0:T(8,128)S(1)} %bitcast.17, f32[64,128]{1,0:T(8,128)S(1)} %bitcast.18, s32[1,384]{1,0:T(1,128)S(1)} %bitcast.20, s32[1,768]{1,0:T(1,128)S(1)} %copy-done.6, f32[1,19]{1,0:T(1,128)S(1)} %copy-done.9, ...), custom_call_target="tpu_custom_call" | custom-call | tf_op jit(solution)/shard_map/pooled/pallas_call | solution.py:301
  71.4 10.4 %all-to-all-start.1 = ((f32[8,8,640]{2,1,0:T(8,128)}), f32[8,8,640]{2,1,0:T(8,128)S(1)}, u32[]{:S(2)}, u32[]{:S(2)}) async-start(f32[8,8,640]{2,1,0:T(8,128)} %bitcast.9), calls=%async_computation.1 | async-start | bytes 327680 | tf_op jit(solution)/shard_map/all_to_all | solution.py:313
  81.9 6.0 %all-to-all-done.1 = f32[8,8,640]{2,1,0:T(8,128)S(1)} async-done(((f32[8,8,640]{2,1,0:T(8,128)}), f32[8,8,640]{2,1,0:T(8,128)S(1)}, u32[]{:S(2)}, u32[]{:S(2)}) %all-to-all-start.1) | async-done | bytes 163872 | tf_op jit(solution)/shard_map/all_to_all | solution.py:313
  87.8 37.9 %all-gather.2 = f32[64,640]{1,0:T(8,128)S(1)} all-gather(f32[8,640]{1,0:T(8,128)S(1)} %reduce_sum.28), channel_id=4, replica_groups=mesh['far'=8,'near'=4,'core'=2,'ty'=4,'tx'=4] {'far'}, dimensions={0}, use_global_device_ids=true | all-gather | bytes 184320 | tf_op jit(solution)/shard_map/all_gather | solution.py:314
  125.7 21.4 %all_gather.27.pooled_ref = f32[64,640]{1,0:T(8,128)S(1)} all-gather(f32[8,640]{1,0:T(8,128)S(1)} %bitcast_reduce_fusion), channel_id=1, replica_groups=mesh['far'=8,'near'=4,'core'=2,'ty'=4,'tx'=4] {'near','core'}, dimensions={0}, use_global_device_ids=true | all-gather | bytes 184320 | tf_op jit(solution)/shard_map/all_gather | solution.py:315
  147.1 1.6 %grads.1 = (f32[1,128]{1,0:T(1,128)}, bf16[384,512]{1,0:T(8,128)(2,1)}, f32[19,512]{1,0:T(8,128)}, f32[1,512]{1,0:T(1,128)}) custom-call(s32[1]{0:T(128)} %bitcast.me_ref, f32[64,640]{1,0:T(8,128)S(1)} %all_gather.27.pooled_ref, f32[24,384]{1,0:T(8,128)S(1)} %get-tuple-element.15.kept_ref, s32[1,384]{1,0:T(1,128)S(1)} %bitcast.21, ...), custom_call_target="tpu_custom_call" | custom-call | tf_op jit(solution)/shard_map/grads/pallas_call | solution.py:317
  (15 shorter events, 0.1 us)
Async XLA Ops:
  1.3 0.7 copy-start.3
  2.0 0.7 copy-start.5
  3.5 66.3 %all-to-all-start = ((f32[64,1,128]{2,1,0:T(1,128)}), f32[64,1,128]{2,1,0:T(1,128)S(1)}, u32[]{:S(2)}, u32[]{:S(2)}) async-start(f32[64,1,128]{2,1,0:T(1,128)} %bitcast.7), calls=%async_computation | async-start | bytes 65536 | tf_op jit(solution)/shard_map/all_to_all | solution.py:267
  34.7 1.2 copy-start
  35.9 2.1 %copy-start.2 = (bf16[384,5120]{1,0:T(8,128)(2,1)S(1)}, bf16[384,5120]{1,0:T(8,128)(2,1)}, u32[]{:S(2)}) copy-start(bf16[384,5120]{1,0:T(8,128)(2,1)} %hidden_ref.1) | copy-start | bytes 11796484
  38.0 0.7 copy-start.7
  38.7 31.1 %copy-start.1 = (bf16[1024,512]{1,0:T(8,128)(2,1)S(1)}, bf16[1024,512]{1,0:T(8,128)(2,1)}, u32[]{:S(2)}) copy-start(bf16[1024,512]{1,0:T(8,128)(2,1)} %text_ref.3) | copy-start | bytes 3145732
  38.7 31.1 %copy-start.4 = (s32[384,1]{0,1:T(1,128)S(1)}, s32[384,1]{0,1:T(1,128)}, u32[]{:S(2)}) copy-start(s32[384,1]{0,1:T(1,128)} %param.15) | copy-start | bytes 4612
  38.7 31.1 %copy-start.6 = (s32[1,768]{1,0:T(1,128)S(1)}, s32[1,768]{1,0:T(1,128)}, u32[]{:S(2)}) copy-start(s32[1,768]{1,0:T(1,128)} %rows_ref.3) | copy-start | bytes 9220
  38.7 31.1 %copy-start.9 = (f32[1,19]{1,0:T(1,128)S(1)}, f32[1,19]{1,0:T(1,128)}, u32[]{:S(2)}) copy-start(f32[1,19]{1,0:T(1,128)} %targets_ref.1) | copy-start | bytes 232
  38.7 43.1 %copy-start.10 = (s32[64,19]{0,1:T(8,128)S(1)}, s32[64,19]{0,1:T(8,128)}, u32[]{:S(2)}) copy-start(s32[64,19]{0,1:T(8,128)} %param.18) | copy-start | bytes 14596
  38.8 108.3 %copy-start.8 = (f32[512]{0:T(512)S(1)}, f32[512]{0:T(512)}, u32[]{:S(2)}) copy-start(f32[512]{0:T(512)} %param.13) | copy-start | bytes 6148
  71.4 16.4 %all-to-all-start.1 = ((f32[8,8,640]{2,1,0:T(8,128)}), f32[8,8,640]{2,1,0:T(8,128)S(1)}, u32[]{:S(2)}, u32[]{:S(2)}) async-start(f32[8,8,640]{2,1,0:T(8,128)} %bitcast.9), calls=%async_computation.1 | async-start | bytes 327680 | tf_op jit(solution)/shard_map/all_to_all | solution.py:313

commit v4 on v3

--- a/solution.py
+++ b/solution.py
@@ -14,11 +14,12 @@
 EPSILON = 1e-06
 LANES = 128
 K_ROWS = 24
-TARGET_AT = 32
+SIDE = 32
 VMEM = pltpu.CompilerParams(vmem_limit_bytes=48 * 2**20)
 EXACT = lax.Precision.HIGHEST
 LAST = (((1,), (1,)), ((), ()))
 FIRST = (((0,), (0,)), ((), ()))
+ALONG = (((1,), (0,)), ((), ()))
 
 
 def iota(shape, dim):
@@ -40,7 +41,28 @@
     return lax.dot_general(a, b, dims, precision=EXACT, preferred_element_type=jnp.float32)
 
 
-def flags_kernel(cap, length_ref, owner_ref, rows_ref, out_ref):
+def target_lane(cap):
+    return -(-(cap + 2) // 8) * 8
+
+
+def packed(pooled, reward):
+    terms = [term.astype(jnp.float32) for term in in_three(reward)]
+    terms.append(jnp.zeros((reward.shape[0], LANES - 3 * SIDE), jnp.float32))
+    side = jnp.concatenate(terms, axis=1)
+    return jnp.concatenate([pooled, side], axis=1).astype(jnp.bfloat16)
+
+
+def rewards_of(side):
+    return side[:, :SIDE] + side[:, SIDE : 2 * SIDE] + side[:, 2 * SIDE : 3 * SIDE]
+
+
+def padded(ref, scratch):
+    scratch[...] = jnp.zeros_like(scratch)
+    scratch[: ref.shape[0]] = ref[...]
+    return scratch[...]
+
+
+def flags_kernel(cap, length_ref, owner_ref, rows_ref, targets_ref, out_ref):
     groups = out_ref.shape[0]
     slots = rows_ref.shape[1]
     length = length_ref[0]
@@ -56,10 +78,14 @@
     lane = iota((groups, LANES), 1)
     flags = jnp.where(lane == cap, count, flags)
     out_ref[...] = jnp.where(lane == cap + 1, length.astype(jnp.float32), flags)
+    first = target_lane(cap)
+    objectives = targets_ref.shape[1]
+    out_ref[:, first : first + objectives] = jnp.broadcast_to(
+        targets_ref[...], (groups, objectives)
+    )
 
 
 def stats_kernel(
-    objectives,
     after_ref,
     hidden_ref,
     weight_ref,
@@ -68,12 +94,26 @@
     head_ref,
     visual_ref,
     stats_ref,
-    total,
-    stats,
+    hidden,
+    weight,
+    text,
+    head,
+    arrived,
 ):
-    step = pl.program_id(0)
-    tokens = total.shape[0]
-    gained = jnp.concatenate(in_three(gain_ref[...] * head_ref[...]), axis=0)
+    chunks, tokens, depth = hidden.shape
+    objectives = head_ref.shape[0]
+    copies = [pltpu.make_async_copy(text_ref, text, arrived.at[0])]
+    for i in range(chunks):
+        part = pl.ds(i * depth, depth)
+        copies.append(
+            pltpu.make_async_copy(hidden_ref.at[:, part], hidden.at[i], arrived.at[2 * i + 1])
+        )
+        copies.append(
+            pltpu.make_async_copy(weight_ref.at[part, :], weight.at[i], arrived.at[2 * i + 2])
+        )
+    for copy in copies:
+        copy.start()
+    gained = jnp.concatenate(in_three(gain_ref[...] * padded(head_ref, head)), axis=0)
 
     def of_rows(x):
         parts = dot32(gained, x, LAST)
@@ -86,25 +126,17 @@
         squares = dot32(ones, high, LAST) + dot32(ones, low, LAST)
         return jnp.where(iota(value.shape, 0) == objectives, squares, value)
 
-    part = dot32(hidden_ref[...], weight_ref[...], (((1,), (0,)), ((), ())))
-
-    @pl.when(step == 0)
-    def _():
-        total[...] = part
-
-    @pl.when(step > 0)
-    def _():
-        total[...] += part
-
-    rows = text_ref.shape[0]
-    stats[:, pl.ds(pl.multiple_of(tokens + step * rows, LANES), rows)] = of_rows(text_ref[...])
-
-    @pl.when(step == pl.num_programs(0) - 1)
-    def _():
-        visual = total[...].astype(jnp.bfloat16)
-        visual_ref[...] = visual
-        stats[:, :tokens] = of_rows(visual)
-        stats_ref[...] = stats[...]
+    copies[0].wait()
+    stats_ref[:, tokens:] = of_rows(text[...])
+    total = None
+    for i in range(chunks):
+        copies[2 * i + 1].wait()
+        copies[2 * i + 2].wait()
+        part = dot32(hidden[i], weight[i], ALONG)
+        total = part if total is None else total + part
+    visual = total.astype(jnp.bfloat16)
+    visual_ref[...] = visual
+    stats_ref[:, :tokens] = of_rows(visual)
 
 
 def pooled_kernel(
@@ -117,7 +149,6 @@
     flags_ref,
     owner_ref,
     rows_ref,
-    targets_ref,
     visual_ref,
     text_ref,
     pooled_ref,
@@ -136,7 +167,7 @@
     owned = owner_ref[...] == iota((groups, tokens), 0)
     member = owned.astype(jnp.bfloat16)
     before = (iota((tokens, tokens), 0) < iota((tokens, tokens), 1)).astype(jnp.bfloat16)
-    earlier = dot32(member, before, (((1,), (0,)), ((), ())))
+    earlier = dot32(member, before, ALONG)
     rank = jnp.sum(jnp.where(owned, earlier, 0.0), axis=0, keepdims=True)
     told = dot_exact(flags, owned.astype(jnp.float32), FIRST)
     at = iota(told.shape, 0)
@@ -160,13 +191,12 @@
     stays = (iota((1, positions), 1) < length) & (replaced < 0.5)
     text_weight = jnp.where(stays, inv[:, tokens:], 0.0) / length.astype(jnp.float32)
 
-    along = (((1,), (0,)), ((), ()))
     spread = jnp.where(owned, token_weight, 0.0)
-    three = dot32(jnp.concatenate(in_three(spread), axis=0), visual_ref[...], along)
+    three = dot32(jnp.concatenate(in_three(spread), axis=0), visual_ref[...], ALONG)
     pooled = three[:groups] + three[groups : 2 * groups] + three[2 * groups :]
     reward = dot_exact(spread, stats[:, :tokens], LAST)
     split = jnp.concatenate(in_three(jnp.broadcast_to(text_weight, (16, positions))), axis=0)
-    text_three = dot32(split, text_ref[...], along)
+    text_three = dot32(split, text_ref[...], ALONG)
     text_pooled = text_three[0:1] + text_three[16:17] + text_three[32:33]
     text_reward = dot_exact(
         jnp.broadcast_to(text_weight, (8, positions)), stats[:, tokens:], LAST
@@ -174,21 +204,35 @@
     mine = iota((groups, 1), 0) == me_ref[0]
     pooled_ref[:, :width] = pooled + jnp.where(mine, text_pooled, 0.0)
     reward = reward + jnp.where(mine, text_reward, 0.0)
-    target = jnp.where(mine, targets_ref[...], 0.0)
     pooled_ref[:, width:] = jnp.zeros((groups, LANES), jnp.float32)
     pooled_ref[:, width : width + objectives] = reward[:, :objectives]
-    pooled_ref[:, width + TARGET_AT : width + TARGET_AT + objectives] = target
     kept = jnp.where(iota((K_ROWS, tokens), 0) == objectives, token_weight, stats[:, :tokens])
     factor = token_weight * token_inv * token_inv / features
     kept_ref[...] = jnp.where(iota((K_ROWS, tokens), 0) == objectives + 1, factor, kept)
 
 
+def fold_kernel(parts_ref, out_ref):
+    total = parts_ref[0].astype(jnp.float32)
+    for part in range(1, parts_ref.shape[0]):
+        total = total + parts_ref[part].astype(jnp.float32)
+    width = total.shape[1] - LANES
+    joined, side = total[:, :width], total[:, width:]
+    if out_ref.dtype == jnp.bfloat16:
+        once = packed(joined, side[:, :SIDE])
+    else:
+        spare = jnp.zeros((side.shape[0], LANES - SIDE), jnp.float32)
+        once = jnp.concatenate([joined, rewards_of(side), spare], axis=1)
+    for copy in range(out_ref.shape[0]):
+        out_ref[copy] = once
+
+
 def grads_kernel(
-    objectives,
+    cap,
     scale,
     me_ref,
     pooled_ref,
     kept_ref,
+    flags_ref,
     owner_ref,
     visual_ref,
     labels_ref,
@@ -198,27 +242,29 @@
     visual_grad_ref,
     head_grad_ref,
     gain_grad_ref,
+    marks,
+    head_all,
 ):
     tokens, width = visual_ref.shape
-    groups = pooled_ref.shape[0]
+    groups = flags_ref.shape[0]
+    objectives = labels_ref.shape[0]
     z = pooled_ref[:, :width]
     rest = pooled_ref[:, width:]
     mine = iota(rest.shape, 0) == me_ref[0]
     reward_ref[...] = jnp.sum(jnp.where(mine, rest, 0.0), axis=0, keepdims=True)
-    turned = rest.T
-    labels = labels_ref[...].astype(jnp.float32)
+    first = target_lane(cap)
+    error = rest.T[:K_ROWS] - flags_ref[...].T[first : first + K_ROWS]
+    labels = padded(labels_ref, marks).astype(jnp.float32)
     count = jnp.maximum(jnp.sum(labels, axis=1, keepdims=True), 1.0)
-    error = turned[:K_ROWS] - turned[TARGET_AT : TARGET_AT + K_ROWS]
     cot = scale * labels * error / count
     gain = gain_ref[...]
-    head = head_ref[...]
-    along = (((1,), (0,)), ((), ()))
-    head_grad_ref[...] = (gain * dot_exact(cot, z, along))[:objectives]
+    head = padded(head_ref, head_all)
+    head_grad_ref[...] = (gain * dot_exact(cot, z, ALONG))[:objectives]
     direction = dot_exact(cot, head, FIRST)
     gain_grad_ref[...] = jnp.sum(z * direction, axis=0, keepdims=True)
     owned = owner_ref[...] == iota((groups, tokens), 0)
     kept = kept_ref[...]
-    own_cot = dot_exact(cot, owned.astype(jnp.float32), along)
+    own_cot = dot_exact(cot, owned.astype(jnp.float32), ALONG)
     is_value = iota(kept.shape, 0) < objectives
     row_dot = jnp.sum(jnp.where(is_value, kept * own_cot, 0.0), axis=0, keepdims=True)
     weight = kept[objectives : objectives + 1]
@@ -236,8 +282,23 @@
     return [pl.BlockSpec(memory_space=pltpu.VMEM)] * count
 
 
+def in_hbm(array):
+    return pltpu.with_memory_space_constraint(array, pltpu.HBM)
+
+
 def scalars(count):
     return [pl.BlockSpec(memory_space=pltpu.SMEM)] * count
+
+
+def folded(parts, copies, kind, name):
+    return pl.pallas_call(
+        fold_kernel,
+        out_shape=jax.ShapeDtypeStruct((copies, *parts.shape[1:]), kind),
+        in_specs=whole(1),
+        out_specs=pl.BlockSpec(memory_space=pltpu.VMEM),
+        compiler_params=VMEM,
+        name=f"fold_{name}",
+    )(parts)
 
 
 def on_device(
@@ -253,49 +314,43 @@
     me = lax.axis_index(GRP).astype(jnp.int32).reshape(1)
     owners = owner.reshape(1, tokens)
     gain_row = gain.reshape(1, width)
-    head = jnp.pad(head_weight.T, ((0, K_ROWS - objectives), (0, 0)))
-    marks = jnp.pad(labels.T, ((0, K_ROWS - objectives), (0, 0)))
+    head = head_weight.T
+    marks = labels.T
 
     flags = pl.pallas_call(
         functools.partial(flags_kernel, cap),
         out_shape=jax.ShapeDtypeStruct((groups, LANES), jnp.float32),
-        in_specs=scalars(1) + whole(2),
+        in_specs=scalars(1) + whole(3),
         out_specs=pl.BlockSpec(memory_space=pltpu.VMEM),
         compiler_params=VMEM,
         name="flags",
-    )(lengths, owners, vis_row)
+    )(lengths, in_hbm(owners), in_hbm(vis_row), in_hbm(targets))
     told = lax.all_to_all(
         flags.reshape(groups, 1, LANES), GRP, split_axis=0, concat_axis=0, tiled=True
     ).reshape(groups, LANES)
 
-    steps = 8
+    chunks = 5
     rows = tokens + positions
     visual, stats = pl.pallas_call(
-        functools.partial(stats_kernel, objectives),
-        grid=(steps,),
+        stats_kernel,
         out_shape=(
             jax.ShapeDtypeStruct((tokens, width), jnp.bfloat16),
             jax.ShapeDtypeStruct((K_ROWS, rows), jnp.float32),
         ),
-        in_specs=[
-            pl.BlockSpec(memory_space=pl.ANY),
-            pl.BlockSpec((tokens, depth // steps), lambda i: (0, i)),
-            pl.BlockSpec((depth // steps, width), lambda i: (i, 0)),
-            pl.BlockSpec((positions // steps, width), lambda i: (i, 0)),
-            pl.BlockSpec((1, width), lambda i: (0, 0)),
-            pl.BlockSpec((K_ROWS, width), lambda i: (0, 0)),
-        ],
-        out_specs=(
-            pl.BlockSpec((tokens, width), lambda i: (0, 0)),
-            pl.BlockSpec((K_ROWS, rows), lambda i: (0, 0)),
-        ),
+        in_specs=[pl.BlockSpec(memory_space=pl.ANY)]
+        + [pl.BlockSpec(memory_space=pltpu.HBM)] * 3
+        + whole(2),
+        out_specs=tuple(whole(2)),
         scratch_shapes=[
-            pltpu.VMEM((tokens, width), jnp.float32),
-            pltpu.VMEM((K_ROWS, rows), jnp.float32),
+            pltpu.VMEM((chunks, tokens, depth // chunks), jnp.bfloat16),
+            pltpu.VMEM((chunks, depth // chunks, width), jnp.bfloat16),
+            pltpu.VMEM((positions, width), jnp.bfloat16),
+            pltpu.VMEM((K_ROWS, width), jnp.float32),
+            pltpu.SemaphoreType.DMA((2 * chunks + 1,)),
         ],
         compiler_params=VMEM,
         name="stats",
-    )(flags, hidden, merge_weight, text_embed, gain_row, head)
+    )(flags, in_hbm(hidden), in_hbm(merge_weight), in_hbm(text_embed), in_hbm(gain_row), in_hbm(head))
     stats = lax.all_gather(jnp.sum(lax.all_gather(stats, "tx"), axis=0), "ty")
 
     pooled, kept = pl.pallas_call(
@@ -304,29 +359,36 @@
             jax.ShapeDtypeStruct((groups, width + LANES), jnp.float32),
             jax.ShapeDtypeStruct((K_ROWS, tokens), jnp.float32),
         ),
-        in_specs=scalars(2) + whole(7),
+        in_specs=scalars(2) + whole(6),
         out_specs=tuple(whole(2)),
         compiler_params=VMEM,
         name="pooled",
-    )(me, lengths, stats, told, owners, vis_row, targets, visual, text_embed)
+    )(me, lengths, stats, told, owners, vis_row, visual, text_embed)
     block = pooled.reshape(near, groups // near, width + LANES)
-    block = jnp.sum(lax.all_to_all(block, NEAR, split_axis=0, concat_axis=0, tiled=True), axis=0)
-    block = jnp.sum(lax.all_gather(block, "far"), axis=0)
-    pooled = lax.all_gather(block, NEAR, tiled=True)
+    block = lax.all_to_all(block, NEAR, split_axis=0, concat_axis=0, tiled=True)
+    block = folded(block, lax.axis_size("far"), jnp.bfloat16, "near")
+    block = lax.all_to_all(block, "far", split_axis=0, concat_axis=0, tiled=True)
+    block = folded(block, near, jnp.float32, "far")
+    block = lax.all_to_all(block, NEAR, split_axis=0, concat_axis=0, tiled=True)
+    pooled = block.reshape(groups, width + LANES)
 
     reward, visual_grad, head_grad, gain_grad = pl.pallas_call(
-        functools.partial(grads_kernel, objectives, scale),
+        functools.partial(grads_kernel, cap, scale),
         out_shape=(
             jax.ShapeDtypeStruct((1, LANES), jnp.float32),
             jax.ShapeDtypeStruct((tokens, width), jnp.bfloat16),
             jax.ShapeDtypeStruct((objectives, width), jnp.float32),
             jax.ShapeDtypeStruct((1, width), jnp.float32),
         ),
-        in_specs=scalars(1) + whole(7),
+        in_specs=scalars(1) + whole(8),
         out_specs=tuple(whole(4)),
+        scratch_shapes=[
+            pltpu.VMEM((K_ROWS, groups), jnp.int32),
+            pltpu.VMEM((K_ROWS, width), jnp.float32),
+        ],
         compiler_params=VMEM,
         name="grads",
-    )(me, pooled, kept, owners, visual, marks, gain_row, head)
+    )(me, pooled, kept, told, owners, visual, marks, gain_row, head)
     return reward[:, :objectives], visual_grad, head_grad.T, gain_grad.reshape(width)
 
 

time: 149 us -> 136 us (0.913)
  blocking collectives: 81.1 us -> 93 us
  starting transfers between devices: 40.8 us -> 30.4 us
  local copies, waits for them, and re-layouts: 6.22 us -> 0.04 us
  waiting for transfers between devices: 5.98 us -> 0.01 us
  Pallas kernels: 13.2 us -> 10.5 us
    all_to_all x0 -> x3, blocking collectives: none -> 70.8 us  [the longest x1 41.3 us: on_device(): lax.all_to_all(block, 'far', split_axis=0, concat_axis=0, tiled=True)]
    all_gather x2 -> x0, blocking collectives: 59.2 us -> none  [the longest x1 37.9 us: on_device(): block = jnp.sum(lax.all_gather(block, 'far'), axis=0)]
    all_to_all x1 -> x0, starting transfers between devices: 10.4 us -> none  [on_device(): lax.all_to_all(block, NEAR, split_axis=0, concat_axis=0, tiled=True)]
    all_to_all x1 -> x0, waiting for transfers between devices: 5.97 us -> none  [on_device(): lax.all_to_all(block, NEAR, split_axis=0, concat_axis=0, tiled=True)]
    unnamed x22 -> x12, local copies, waits for them, and re-layouts: 5.4 us -> 0.04 us
    pallas_call x2 -> x4, Pallas kernels: 10.8 us -> 8.02 us  [the longest x1 6.26 us: on_device(): pl.pallas_call(stats_kernel, out_shape=(jax.ShapeDtypeStruct((tokens, wid...]
  transfers between devices with their start and end apart: 2 -> 1, of which waited for: 1 -> 0; matrix products, arithmetic and copies ran while one was open for 1% -> 0% of each run, Pallas kernels for 6% -> 5%
where the time goes in v4:
time: 136 us; the launch traced here: 135 us
  blocking collectives  93 us (68%)
  starting transfers between devices  30.4 us (22%)
  Pallas kernels  10.5 us (8%)
  between operations  1.37 us (1%)
    all_to_all x1, blocking collectives, on_device(): lax.all_to_all(block, 'far', split_axis=0, concat_axis=0, tiled=True)  41.3 us
    all_to_all x1, starting transfers between devices, on_device(): lax.all_to_all(flags.reshape(groups, 1, LANES), GRP, split_axis=0, concat...  30.4 us
    all_to_all x2, blocking collectives, on_device(): block = lax.all_to_all(block, NEAR, split_axis=0, concat_axis=0, tiled=True)  29.4 us
    all_gather x2, blocking collectives, on_device(): stats = lax.all_gather(jnp.sum(lax.all_gather(stats, 'tx'), axis=0), 'ty')  22.3 us
    pallas_call x1, Pallas kernels, on_device(): pl.pallas_call(stats_kernel, out_shape=(jax.ShapeDtypeStruct((tokens, wid...  6.26 us
  transfers between devices with their start and end apart: 1, of which 0 were waited for; matrix products, arithmetic and copies ran while one was open for 0% of the time, Pallas kernels for 5%

profile of v4, /device:TPU:1, one launch (start us, length us, event | category | flops | bytes accessed | tf_op | source)
XLA Modules:
  0.0 135.4 jit_solution(15357691700874102375)
XLA Ops:
  1.3 1.6 %flags.1.after_ref = f32[64,128]{1,0:T(8,128)} custom-call(s32[1]{0:T(128)S(6)} %copy.15.length_ref, s32[1,384]{1,0:T(1,128)} %bitcast.23, s32[1,768]{1,0:T(1,128)} %rows_ref.3, f32[1,19]{1,0:T(1,128)} %targets_ref.1), custom_call_target="tpu_custom_call" | custom-call | tf_op jit(solution)/shard_map/flags/pallas_call | solution.py:320
  2.8 30.4 %all-to-all-start = ((f32[64,1,128]{2,1,0:T(1,128)}), f32[64,1,128]{2,1,0:T(1,128)S(1)}, u32[]{:S(2)}, u32[]{:S(2)}) async-start(f32[64,1,128]{2,1,0:T(1,128)} %bitcast.7), calls=%async_computation | async-start | bytes 65536 | tf_op jit(solution)/shard_map/all_to_all | solution.py:328
  33.2 0.0 copy-start
  33.3 0.0 copy-start.2
  33.3 0.0 copy-start.3
  33.3 6.3 %stats.1 = (bf16[384,512]{1,0:T(8,128)(2,1)S(1)}, f32[24,1408]{1,0:T(8,128)S(1)}) custom-call(f32[64,128]{1,0:T(8,128)} %flags.1.after_ref, bf16[384,5120]{1,0:T(8,128)(2,1)} %hidden_ref.1, bf16[5120,512]{1,0:T(8,128)(2,1)} %weight_ref.1, bf16[1024,512]{1,0:T(8,128)(2,1)} %text_ref.3, f32[1,512]{1,0:T(1,128)} %bitcast.27, f32[19,512]{1,0:T(8,128)} %bitcast.20), custom_call_target="tpu_custom_call" | custom-call | tf_op jit(solution)/shard_map/stats/pallas_call | solution.py:334
  39.5 0.0 copy-start.1
  39.6 0.0 copy-start.4
  39.6 0.0 copy-start.5
  39.6 11.5 %all-gather = f32[96,1408]{1,0:T(8,128)S(1)} all-gather(f32[24,1408]{1,0:T(8,128)S(1)} %get-tuple-element.12), channel_id=2, replica_groups=mesh['far'=8,'near'=4,'core'=2,'ty'=4,'tx'=4] {'tx'}, dimensions={0}, use_global_device_ids=true | all-gather | bytes 675840 | tf_op jit(solution)/shard_map/all_gather | solution.py:354
  51.1 10.7 %all-gather.1 = f32[96,1408]{1,0:T(8,128)S(1)} all-gather(f32[24,1408]{1,0:T(8,128)S(1)} %reduce_sum.9), channel_id=3, replica_groups=mesh['far'=8,'near'=4,'core'=2,'ty'=4,'tx'=4] {'ty'}, dimensions={0}, use_global_device_ids=true | all-gather | bytes 675840 | tf_op jit(solution)/shard_map/all_gather | solution.py:354
  61.9 0.0 all-to-all-done
  61.9 0.0 copy-done
  61.9 0.0 copy-done.2
  61.9 0.0 copy-done.3
  61.9 1.0 pooled.1
  62.9 15.9 %all_to_all.20.parts_ref = f32[8,8,640]{2,1,0:T(8,128)S(1)} all-to-all(f32[8,8,640]{2,1,0:T(8,128)S(1)} %bitcast.22), channel_id=1, replica_groups=mesh['far'=8,'near'=4,'core'=2,'ty'=4,'tx'=4] {'near','core'}, dimensions={0} | all-to-all | bytes 327680 | tf_op jit(solution)/shard_map/all_to_all | solution.py:368
  78.8 0.1 fold_near.1
  78.9 41.3 %all_to_all.21.parts_ref = bf16[8,8,640]{2,1,0:T(8,128)(2,1)S(1)} all-to-all(bf16[8,8,640]{2,1,0:T(8,128)(2,1)S(1)} %fold_near.1), channel_id=1, replica_groups=mesh['far'=8,'near'=4,'core'=2,'ty'=4,'tx'=4] {'far'}, dimensions={0} | all-to-all | bytes 163840 | tf_op jit(solution)/shard_map/all_to_all | solution.py:370
  120.2 0.1 fold_far.1
  120.3 13.5 %all_to_all.22 = f32[8,8,640]{2,1,0:T(8,128)S(1)} all-to-all(f32[8,8,640]{2,1,0:T(8,128)S(1)} %fold_far.1), channel_id=1, replica_groups=mesh['far'=8,'near'=4,'core'=2,'ty'=4,'tx'=4] {'near','core'}, dimensions={0} | all-to-all | bytes 327680 | tf_op jit(solution)/shard_map/all_to_all | solution.py:372
  133.8 0.0 copy-done.1
  133.8 0.0 copy-done.4
  133.8 1.6 %grads.1 = (f32[1,128]{1,0:T(1,128)}, bf16[384,512]{1,0:T(8,128)(2,1)}, f32[19,512]{1,0:T(8,128)}, f32[1,512]{1,0:T(1,128)}) custom-call(s32[1]{0:T(128)} %bitcast.me_ref, f32[64,640]{1,0:T(8,128)S(1)} %bitcast.17, f32[24,384]{1,0:T(8,128)S(1)} %get-tuple-element.15.kept_ref, f32[64,128]{1,0:T(8,128)S(1)} %bitcast.19, s32[1,384]{1,0:T(1,128)S(1)} %bitcast.25, ...), custom_call_target="tpu_custom_call" | custom-call | tf_op jit(solution)/shard_map/grads/pallas_call | solution.py:375
  (2 shorter events, 0.0 us)
Async XLA Ops:
  2.8 59.1 %all-to-all-start = ((f32[64,1,128]{2,1,0:T(1,128)}), f32[64,1,128]{2,1,0:T(1,128)S(1)}, u32[]{:S(2)}, u32[]{:S(2)}) async-start(f32[64,1,128]{2,1,0:T(1,128)} %bitcast.7), calls=%async_computation | async-start | bytes 65536 | tf_op jit(solution)/shard_map/all_to_all | solution.py:328
  33.2 28.7 %copy-start = (bf16[1024,512]{1,0:T(8,128)(2,1)S(1)}, bf16[1024,512]{1,0:T(8,128)(2,1)}, u32[]{:S(2)}) copy-start(bf16[1024,512]{1,0:T(8,128)(2,1)} %text_ref.3) | copy-start | bytes 3145732
  33.3 28.6 %copy-start.2 = (s32[384,1]{0,1:T(1,128)S(1)}, s32[384,1]{0,1:T(1,128)}, u32[]{:S(2)}) copy-start(s32[384,1]{0,1:T(1,128)} %param.15) | copy-start | bytes 4612
  33.3 28.6 %copy-start.3 = (s32[1,768]{1,0:T(1,128)S(1)}, s32[1,768]{1,0:T(1,128)}, u32[]{:S(2)}) copy-start(s32[1,768]{1,0:T(1,128)} %rows_ref.3) | copy-start | bytes 9220
  39.5 94.3 %copy-start.1 = (f32[512,19]{0,1:T(8,128)S(1)}, f32[512,19]{0,1:T(8,128)}, u32[]{:S(2)}) copy-start(f32[512,19]{0,1:T(8,128)} %param.14) | copy-start | bytes 116740
  39.6 94.3 %copy-start.4 = (s32[64,19]{0,1:T(8,128)S(1)}, s32[64,19]{0,1:T(8,128)}, u32[]{:S(2)}) copy-start(s32[64,19]{0,1:T(8,128)} %param.18) | copy-start | bytes 14596
  39.6 94.3 %copy-start.5 = (f32[512]{0:T(512)S(1)}, f32[512]{0:T(512)}, u32[]{:S(2)}) copy-start(f32[512]{0:T(512)} %param.13) | copy-start | bytes 6148

commit v5 on v4

--- a/solution.py
+++ b/solution.py
@@ -60,6 +60,25 @@
     scratch[...] = jnp.zeros_like(scratch)
     scratch[: ref.shape[0]] = ref[...]
     return scratch[...]
+
+
+def tight_lanes(rows):
+    return -(-rows // (2 * LANES)) * LANES
+
+
+def tight(stats):
+    rows = stats.shape[1]
+    half = tight_lanes(rows)
+    last = jnp.concatenate([stats[16:20, :half], stats[16:20, rows - half :]], axis=0)
+    return jnp.concatenate([stats[:8], stats[8:16], last], axis=1)
+
+
+def loose(packed_stats, rows):
+    half = tight_lanes(rows)
+    last = packed_stats[:, 2 * rows :]
+    last = jnp.concatenate([last[:4, :half], last[4:, 2 * half - rows :]], axis=1)
+    last = jnp.concatenate([last, jnp.zeros_like(last)], axis=0)
+    return jnp.concatenate([packed_stats[:, :rows], packed_stats[:, rows : 2 * rows], last], axis=0)
 
 
 def flags_kernel(cap, length_ref, owner_ref, rows_ref, targets_ref, out_ref):
@@ -120,14 +139,15 @@
         value = parts[:K_ROWS] + parts[K_ROWS : 2 * K_ROWS] + parts[2 * K_ROWS :]
         wide = x.astype(jnp.float32)
         square = wide * wide
-        high = square.astype(jnp.bfloat16)
-        low = (square - high.astype(jnp.float32)).astype(jnp.bfloat16)
-        ones = jnp.ones((K_ROWS, x.shape[1]), jnp.bfloat16)
-        squares = dot32(ones, high, LAST) + dot32(ones, low, LAST)
+        lanes = square[:, :LANES]
+        for at in range(LANES, x.shape[1], LANES):
+            lanes = lanes + square[:, at : at + LANES]
+        terms = jnp.concatenate(in_three(lanes), axis=1)
+        squares = dot32(jnp.ones((K_ROWS, terms.shape[1]), jnp.bfloat16), terms, LAST)
         return jnp.where(iota(value.shape, 0) == objectives, squares, value)
 
     copies[0].wait()
-    stats_ref[:, tokens:] = of_rows(text[...])
+    of_text = of_rows(text[...])
     total = None
     for i in range(chunks):
         copies[2 * i + 1].wait()
@@ -136,7 +156,7 @@
         total = part if total is None else total + part
     visual = total.astype(jnp.bfloat16)
     visual_ref[...] = visual
-    stats_ref[:, :tokens] = of_rows(visual)
+    stats_ref[...] = tight(jnp.concatenate([of_rows(visual), of_text], axis=1))
 
 
 def pooled_kernel(
@@ -161,6 +181,7 @@
     stats = stats_ref[0]
     for part in range(1, stats_ref.shape[0]):
         stats = stats + stats_ref[part]
+    stats = loose(stats, tokens + positions)
     inv = lax.rsqrt(stats[objectives : objectives + 1] / features + EPSILON)
     flags = flags_ref[...]
 
@@ -335,7 +356,7 @@
         stats_kernel,
         out_shape=(
             jax.ShapeDtypeStruct((tokens, width), jnp.bfloat16),
-            jax.ShapeDtypeStruct((K_ROWS, rows), jnp.float32),
+            jax.ShapeDtypeStruct((8, 2 * rows + tight_lanes(rows)), jnp.float32),
         ),
         in_specs=[pl.BlockSpec(memory_space=pl.ANY)]
         + [pl.BlockSpec(memory_space=pltpu.HBM)] * 3

time: 136 us -> 135 us (level)
  transfers between devices with their start and end apart: 1 -> 1, of which waited for: 0 -> 0; matrix products, arithmetic and copies ran while one was open for 0% -> 0% of each run, Pallas kernels for 5% -> 4%
where the time goes in v5:
time: 135 us
  blocking collectives  92.5 us (69%)
  starting transfers between devices  30.4 us (23%)
  Pallas kernels  10.2 us (8%)
  between operations  1.38 us (1%)
    all_to_all x1, blocking collectives, on_device(): lax.all_to_all(block, 'far', split_axis=0, concat_axis=0, tiled=True)  41.4 us
    all_to_all x1, starting transfers between devices, on_device(): lax.all_to_all(flags.reshape(groups, 1, LANES), GRP, split_axis=0, concat...  30.4 us
    all_to_all x2, blocking collectives, on_device(): block = lax.all_to_all(block, NEAR, split_axis=0, concat_axis=0, tiled=True)  29.4 us
    all_gather x2, blocking collectives, on_device(): stats = lax.all_gather(jnp.sum(lax.all_gather(stats, 'tx'), axis=0), 'ty')  21.8 us
    pallas_call x1, Pallas kernels, on_device(): pl.pallas_call(stats_kernel, out_shape=(jax.ShapeDtypeStruct((tokens, wid...  5.96 us
  transfers between devices with their start and end apart: 1, of which 0 were waited for; matrix products, arithmetic and copies ran while one was open for 0% of the time, Pallas kernels for 4%

profile of v5, /device:TPU:1, one launch (start us, length us, event | category | flops | bytes accessed | tf_op | source)
XLA Modules:
  0.0 134.6 jit_solution(9266997904432942924)
XLA Ops:
  1.3 1.6 %flags.1.after_ref = f32[64,128]{1,0:T(8,128)} custom-call(s32[1]{0:T(128)S(6)} %copy.15.length_ref, s32[1,384]{1,0:T(1,128)} %bitcast.24, s32[1,768]{1,0:T(1,128)} %rows_ref.3, f32[1,19]{1,0:T(1,128)} %targets_ref.1), custom_call_target="tpu_custom_call" | custom-call | tf_op jit(solution)/shard_map/flags/pallas_call | solution.py:341
  2.8 30.4 %all-to-all-start = ((f32[64,1,128]{2,1,0:T(1,128)}), f32[64,1,128]{2,1,0:T(1,128)S(1)}, u32[]{:S(2)}, u32[]{:S(2)}) async-start(f32[64,1,128]{2,1,0:T(1,128)} %bitcast.7), calls=%async_computation | async-start | bytes 65536 | tf_op jit(solution)/shard_map/all_to_all | solution.py:349
  33.2 0.0 copy-start
  33.3 0.0 copy-start.2
  33.3 0.0 copy-start.4
  33.3 0.0 copy-start.1
  33.3 0.0 copy-start.3
  33.3 0.0 copy-start.5
  33.3 6.0 %stats.1 = (bf16[384,512]{1,0:T(8,128)(2,1)S(1)}, f32[8,3584]{1,0:T(8,128)S(1)}) custom-call(f32[64,128]{1,0:T(8,128)} %flags.1.after_ref, bf16[384,5120]{1,0:T(8,128)(2,1)} %hidden_ref.1, bf16[5120,512]{1,0:T(8,128)(2,1)} %weight_ref.1, bf16[1024,512]{1,0:T(8,128)(2,1)} %text_ref.3, f32[1,512]{1,0:T(1,128)} %bitcast.28, f32[19,512]{1,0:T(8,128)} %bitcast.21), custom_call_target="tpu_custom_call" | custom-call | tf_op jit(solution)/shard_map/stats/pallas_call | solution.py:355
  39.3 11.2 %all-gather = f32[32,3584]{1,0:T(8,128)S(1)} all-gather(f32[8,3584]{1,0:T(8,128)S(1)} %get-tuple-element.12), channel_id=2, replica_groups=mesh['far'=8,'near'=4,'core'=2,'ty'=4,'tx'=4] {'tx'}, dimensions={0}, use_global_device_ids=true | all-gather | bytes 573440 | tf_op jit(solution)/shard_map/all_gather | solution.py:375
  50.5 10.6 %all-gather.1 = f32[32,3584]{1,0:T(8,128)S(1)} all-gather(f32[8,3584]{1,0:T(8,128)S(1)} %bitcast_reduce_fusion), channel_id=3, replica_groups=mesh['far'=8,'near'=4,'core'=2,'ty'=4,'tx'=4] {'ty'}, dimensions={0}, use_global_device_ids=true | all-gather | bytes 573440 | tf_op jit(solution)/shard_map/all_gather | solution.py:375
  61.1 0.0 all-to-all-done
  61.1 0.0 copy-done
  61.1 0.0 copy-done.2
  61.1 0.0 copy-done.4
  61.1 1.0 pooled.1
  62.1 15.9 %all_to_all.20.parts_ref = f32[8,8,640]{2,1,0:T(8,128)S(1)} all-to-all(f32[8,8,640]{2,1,0:T(8,128)S(1)} %bitcast.23), channel_id=1, replica_groups=mesh['far'=8,'near'=4,'core'=2,'ty'=4,'tx'=4] {'near','core'}, dimensions={0} | all-to-all | bytes 327680 | tf_op jit(solution)/shard_map/all_to_all | solution.py:389
  78.0 0.1 fold_near.1
  78.1 41.4 %all_to_all.21.parts_ref = bf16[8,8,640]{2,1,0:T(8,128)(2,1)S(1)} all-to-all(bf16[8,8,640]{2,1,0:T(8,128)(2,1)S(1)} %fold_near.1), channel_id=1, replica_groups=mesh['far'=8,'near'=4,'core'=2,'ty'=4,'tx'=4] {'far'}, dimensions={0} | all-to-all | bytes 163840 | tf_op jit(solution)/shard_map/all_to_all | solution.py:391
  119.4 0.1 fold_far.1
  119.5 13.5 %all_to_all.22 = f32[8,8,640]{2,1,0:T(8,128)S(1)} all-to-all(f32[8,8,640]{2,1,0:T(8,128)S(1)} %fold_far.1), channel_id=1, replica_groups=mesh['far'=8,'near'=4,'core'=2,'ty'=4,'tx'=4] {'near','core'}, dimensions={0} | all-to-all | bytes 327680 | tf_op jit(solution)/shard_map/all_to_all | solution.py:393
  133.0 0.0 copy-done.1
  133.0 0.0 copy-done.3
  133.0 1.6 %grads.1 = (f32[1,128]{1,0:T(1,128)}, bf16[384,512]{1,0:T(8,128)(2,1)}, f32[19,512]{1,0:T(8,128)}, f32[1,512]{1,0:T(1,128)}) custom-call(s32[1]{0:T(128)} %bitcast.me_ref, f32[64,640]{1,0:T(8,128)S(1)} %bitcast.18, f32[24,384]{1,0:T(8,128)S(1)} %get-tuple-element.15.kept_ref, f32[64,128]{1,0:T(8,128)S(1)} %bitcast.20, s32[1,384]{1,0:T(1,128)S(1)} %bitcast.26, ...), custom_call_target="tpu_custom_call" | custom-call | tf_op jit(solution)/shard_map/grads/pallas_call | solution.py:396
  (2 shorter events, 0.0 us)
Async XLA Ops:
  2.8 58.3 %all-to-all-start = ((f32[64,1,128]{2,1,0:T(1,128)}), f32[64,1,128]{2,1,0:T(1,128)S(1)}, u32[]{:S(2)}, u32[]{:S(2)}) async-start(f32[64,1,128]{2,1,0:T(1,128)} %bitcast.7), calls=%async_computation | async-start | bytes 65536 | tf_op jit(solution)/shard_map/all_to_all | solution.py:349
  33.2 27.8 %copy-start = (bf16[1024,512]{1,0:T(8,128)(2,1)S(1)}, bf16[1024,512]{1,0:T(8,128)(2,1)}, u32[]{:S(2)}) copy-start(bf16[1024,512]{1,0:T(8,128)(2,1)} %text_ref.3) | copy-start | bytes 3145732
  33.3 27.8 %copy-start.2 = (s32[384,1]{0,1:T(1,128)S(1)}, s32[384,1]{0,1:T(1,128)}, u32[]{:S(2)}) copy-start(s32[384,1]{0,1:T(1,128)} %param.15) | copy-start | bytes 4612
  33.3 27.8 %copy-start.4 = (s32[1,768]{1,0:T(1,128)S(1)}, s32[1,768]{1,0:T(1,128)}, u32[]{:S(2)}) copy-start(s32[1,768]{1,0:T(1,128)} %rows_ref.3) | copy-start | bytes 9220
  33.3 99.8 %copy-start.1 = (f32[512,19]{0,1:T(8,128)S(1)}, f32[512,19]{0,1:T(8,128)}, u32[]{:S(2)}) copy-start(f32[512,19]{0,1:T(8,128)} %param.14) | copy-start | bytes 116740
  33.3 99.7 %copy-start.3 = (s32[64,19]{0,1:T(8,128)S(1)}, s32[64,19]{0,1:T(8,128)}, u32[]{:S(2)}) copy-start(s32[64,19]{0,1:T(8,128)} %param.18) | copy-start | bytes 14596
  33.3 99.7 %copy-start.5 = (f32[512]{0:T(512)S(1)}, f32[512]{0:T(512)}, u32[]{:S(2)}) copy-start(f32[512]{0:T(512)} %param.13) | copy-start | bytes 6148

commit v6 on v5

--- a/solution.py
+++ b/solution.py
@@ -347,8 +347,8 @@
         name="flags",
     )(lengths, in_hbm(owners), in_hbm(vis_row), in_hbm(targets))
     told = lax.all_to_all(
-        flags.reshape(groups, 1, LANES), GRP, split_axis=0, concat_axis=0, tiled=True
-    ).reshape(groups, LANES)
+        flags.reshape(groups // near, near, LANES), "far", split_axis=0, concat_axis=0, tiled=True
+    )
 
     chunks = 5
     rows = tokens + positions
@@ -372,6 +372,9 @@
         compiler_params=VMEM,
         name="stats",
     )(flags, in_hbm(hidden), in_hbm(merge_weight), in_hbm(text_embed), in_hbm(gain_row), in_hbm(head))
+    stats, told = lax.optimization_barrier((stats, told))
+    told = lax.all_to_all(told, NEAR, split_axis=1, concat_axis=1, tiled=True)
+    told = told.reshape(groups, LANES)
     stats = lax.all_gather(jnp.sum(lax.all_gather(stats, "tx"), axis=0), "ty")
 
     pooled, kept = pl.pallas_call(

time: 135 us -> 141 us (1.044)
  waiting for transfers between devices: 0.01 us -> 15.9 us
  blocking collectives: 92.5 us -> 78.1 us
  starting transfers between devices: 30.4 us -> 34.1 us
    all_to_all x1 -> x2, waiting for transfers between devices: 0.01 us -> 15.9 us  [the longest x1 15.9 us: on_device(): lax.all_to_all(flags.reshape(groups // near, near, LANES), 'far', split_a...]
    all_to_all x1, blocking collectives: 41.4 us -> 26.8 us  [on_device(): lax.all_to_all(block, 'far', split_axis=0, concat_axis=0, tiled=True)]
    all_to_all x1 -> x2, starting transfers between devices: 30.4 us -> 34.1 us  [the longest x1 28.9 us: on_device(): lax.all_to_all(flags.reshape(groups // near, near, LANES), 'far', split_a...]
  transfers between devices with their start and end apart: 1 -> 2, of which waited for: 0 -> 1; matrix products, arithmetic and copies ran while one was open for 0% -> 0% of each run, Pallas kernels for 4% -> 4%
where the time goes in v6:
time: 141 us; the launch traced here: 140 us
  blocking collectives  78.1 us (55%)
  starting transfers between devices  34.1 us (24%)
  waiting for transfers between devices  15.9 us (11%)
  Pallas kernels  10.2 us (7%)
    all_to_all x2, blocking collectives, on_device(): block = lax.all_to_all(block, NEAR, split_axis=0, concat_axis=0, tiled=True)  30.3 us
    all_to_all x1, starting transfers between devices, on_device(): lax.all_to_all(flags.reshape(groups // near, near, LANES), 'far', split_a...  28.9 us
    all_to_all x1, blocking collectives, on_device(): lax.all_to_all(block, 'far', split_axis=0, concat_axis=0, tiled=True)  26.8 us
    all_gather x2, blocking collectives, on_device(): stats = lax.all_gather(jnp.sum(lax.all_gather(stats, 'tx'), axis=0), 'ty')  21 us
    all_to_all x1, waiting for transfers between devices, on_device(): lax.all_to_all(flags.reshape(groups // near, near, LANES), 'far', split_a...  15.9 us
    pallas_call x1, Pallas kernels, on_device(): pl.pallas_call(stats_kernel, out_shape=(jax.ShapeDtypeStruct((tokens, wid...  5.96 us
    all_to_all x1, starting transfers between devices, on_device(): told = lax.all_to_all(told, NEAR, split_axis=1, concat_axis=1, tiled=True)  5.18 us
  transfers between devices with their start and end apart: 2, of which 1 were waited for; matrix products, arithmetic and copies ran while one was open for 0% of the time, Pallas kernels for 4%

profile of v6, /device:TPU:1, one launch (start us, length us, event | category | flops | bytes accessed | tf_op | source)
XLA Modules:
  0.0 140.4 jit_solution(13409801601702193361)
XLA Ops:
  1.3 1.6 %flags.1.after_ref = f32[64,128]{1,0:T(8,128)} custom-call(s32[1]{0:T(128)S(6)} %copy.20.length_ref, s32[1,384]{1,0:T(1,128)} %bitcast.24, s32[1,768]{1,0:T(1,128)} %rows_ref.3, f32[1,19]{1,0:T(1,128)} %targets_ref.1), custom_call_target="tpu_custom_call" | custom-call | tf_op jit(solution)/shard_map/flags/pallas_call | solution.py:341
  2.8 28.9 %all-to-all-start = ((f32[8,8,128]{2,1,0:T(8,128)}), f32[8,8,128]{2,1,0:T(8,128)S(1)}, u32[]{:S(2)}, u32[]{:S(2)}) async-start(f32[8,8,128]{2,1,0:T(8,128)} %bitcast.4), calls=%async_computation | async-start | bytes 65536 | tf_op jit(solution)/shard_map/all_to_all | solution.py:349
  31.7 0.0 copy-start.2
  31.7 0.0 copy-start.4
  31.8 0.0 copy-start.1
  31.8 0.0 copy-start.3
  31.8 0.0 copy-start.5
  31.8 6.0 %stats.1 = (bf16[384,512]{1,0:T(8,128)(2,1)S(1)}, f32[8,3584]{1,0:T(8,128)S(1)}) custom-call(f32[64,128]{1,0:T(8,128)} %flags.1.after_ref, bf16[384,5120]{1,0:T(8,128)(2,1)} %hidden_ref.1, bf16[5120,512]{1,0:T(8,128)(2,1)} %weight_ref.1, bf16[1024,512]{1,0:T(8,128)(2,1)} %text_ref.3, f32[1,512]{1,0:T(1,128)} %bitcast.28, f32[19,512]{1,0:T(8,128)} %bitcast.21), custom_call_target="tpu_custom_call" | custom-call | tf_op jit(solution)/shard_map/stats/pallas_call | solution.py:355
  37.8 15.9 %all-to-all-done = f32[8,8,128]{2,1,0:T(8,128)S(1)} async-done(((f32[8,8,128]{2,1,0:T(8,128)}), f32[8,8,128]{2,1,0:T(8,128)S(1)}, u32[]{:S(2)}, u32[]{:S(2)}) %all-to-all-start) | async-done | bytes 32800 | tf_op jit(solution)/shard_map/all_to_all | solution.py:349
  53.7 0.6 copy.16
  54.3 5.2 %all-to-all-start.1 = ((f32[8,8,128]{2,0,1:T(8,128)}), f32[8,8,128]{2,0,1:T(8,128)S(1)}, u32[]{:S(2)}, u32[]{:S(2)}) async-start(f32[8,8,128]{2,0,1:T(8,128)} %copy.16), calls=%async_computation.1 | async-start | bytes 65536 | tf_op jit(solution)/shard_map/all_to_all | solution.py:376
  59.5 10.6 %all-gather = f32[32,3584]{1,0:T(8,128)S(1)} all-gather(f32[8,3584]{1,0:T(8,128)S(1)} %get-tuple-element.15), channel_id=2, replica_groups=mesh['far'=8,'near'=4,'core'=2,'ty'=4,'tx'=4] {'tx'}, dimensions={0}, use_global_device_ids=true | all-gather | bytes 573440 | tf_op jit(solution)/shard_map/all_gather | solution.py:378
  70.1 10.4 %all-gather.1 = f32[32,3584]{1,0:T(8,128)S(1)} all-gather(f32[8,3584]{1,0:T(8,128)S(1)} %bitcast_reduce_fusion), channel_id=3, replica_groups=mesh['far'=8,'near'=4,'core'=2,'ty'=4,'tx'=4] {'ty'}, dimensions={0}, use_global_device_ids=true | all-gather | bytes 573440 | tf_op jit(solution)/shard_map/all_gather | solution.py:378
  80.5 0.0 all-to-all-done.1
  80.6 0.0 copy-done
  80.6 0.0 copy-done.2
  80.6 0.0 copy-done.4
  80.6 1.0 pooled.1
  81.6 16.6 %all_to_all.25.parts_ref = f32[8,8,640]{2,1,0:T(8,128)S(1)} all-to-all(f32[8,8,640]{2,1,0:T(8,128)S(1)} %bitcast.23), channel_id=1, replica_groups=mesh['far'=8,'near'=4,'core'=2,'ty'=4,'tx'=4] {'near','core'}, dimensions={0} | all-to-all | bytes 327680 | tf_op jit(solution)/shard_map/all_to_all | solution.py:392
  98.2 0.1 fold_near.1
  98.3 26.8 %all_to_all.26.parts_ref = bf16[8,8,640]{2,1,0:T(8,128)(2,1)S(1)} all-to-all(bf16[8,8,640]{2,1,0:T(8,128)(2,1)S(1)} %fold_near.1), channel_id=1, replica_groups=mesh['far'=8,'near'=4,'core'=2,'ty'=4,'tx'=4] {'far'}, dimensions={0} | all-to-all | bytes 163840 | tf_op jit(solution)/shard_map/all_to_all | solution.py:394
  125.0 0.1 fold_far.1
  125.1 13.7 %all_to_all.27 = f32[8,8,640]{2,1,0:T(8,128)S(1)} all-to-all(f32[8,8,640]{2,1,0:T(8,128)S(1)} %fold_far.1), channel_id=1, replica_groups=mesh['far'=8,'near'=4,'core'=2,'ty'=4,'tx'=4] {'near','core'}, dimensions={0} | all-to-all | bytes 327680 | tf_op jit(solution)/shard_map/all_to_all | solution.py:396
  138.8 1.6 %grads.1 = (f32[1,128]{1,0:T(1,128)}, bf16[384,512]{1,0:T(8,128)(2,1)}, f32[19,512]{1,0:T(8,128)}, f32[1,512]{1,0:T(1,128)}) custom-call(s32[1]{0:T(128)} %bitcast.me_ref, f32[64,640]{1,0:T(8,128)S(1)} %bitcast.18, f32[24,384]{1,0:T(8,128)S(1)} %get-tuple-element.19.kept_ref, f32[64,128]{1,0:T(8,128)S(1)} %bitcast.20, s32[1,384]{1,0:T(1,128)S(1)} %bitcast.26, ...), custom_call_target="tpu_custom_call" | custom-call | tf_op jit(solution)/shard_map/grads/pallas_call | solution.py:399
  (6 shorter events, 0.0 us)
Async XLA Ops:
  2.8 50.9 %all-to-all-start = ((f32[8,8,128]{2,1,0:T(8,128)}), f32[8,8,128]{2,1,0:T(8,128)S(1)}, u32[]{:S(2)}, u32[]{:S(2)}) async-start(f32[8,8,128]{2,1,0:T(8,128)} %bitcast.4), calls=%async_computation | async-start | bytes 65536 | tf_op jit(solution)/shard_map/all_to_all | solution.py:349
  31.7 48.8 %copy-start = (bf16[1024,512]{1,0:T(8,128)(2,1)S(1)}, bf16[1024,512]{1,0:T(8,128)(2,1)}, u32[]{:S(2)}) copy-start(bf16[1024,512]{1,0:T(8,128)(2,1)} %text_ref.3) | copy-start | bytes 3145732
  31.7 48.8 %copy-start.2 = (s32[384,1]{0,1:T(1,128)S(1)}, s32[384,1]{0,1:T(1,128)}, u32[]{:S(2)}) copy-start(s32[384,1]{0,1:T(1,128)} %param.15) | copy-start | bytes 4612
  31.7 48.8 %copy-start.4 = (s32[1,768]{1,0:T(1,128)S(1)}, s32[1,768]{1,0:T(1,128)}, u32[]{:S(2)}) copy-start(s32[1,768]{1,0:T(1,128)} %rows_ref.3) | copy-start | bytes 9220
  31.8 107.0 %copy-start.1 = (f32[512,19]{0,1:T(8,128)S(1)}, f32[512,19]{0,1:T(8,128)}, u32[]{:S(2)}) copy-start(f32[512,19]{0,1:T(8,128)} %param.14) | copy-start | bytes 116740
  31.8 107.0 %copy-start.3 = (s32[64,19]{0,1:T(8,128)S(1)}, s32[64,19]{0,1:T(8,128)}, u32[]{:S(2)}) copy-start(s32[64,19]{0,1:T(8,128)} %param.18) | copy-start | bytes 14596
  31.8 107.0 %copy-start.5 = (f32[512]{0:T(512)S(1)}, f32[512]{0:T(512)}, u32[]{:S(2)}) copy-start(f32[512]{0:T(512)} %param.13) | copy-start | bytes 6148
  54.3 26.2 %all-to-all-start.1 = ((f32[8,8,128]{2,0,1:T(8,128)}), f32[8,8,128]{2,0,1:T(8,128)S(1)}, u32[]{:S(2)}, u32[]{:S(2)}) async-start(f32[8,8,128]{2,0,1:T(8,128)} %copy.16), calls=%async_computation.1 | async-start | bytes 65536 | tf_op jit(solution)/shard_map/all_to_all | solution.py:376

commit v7 on v5

--- a/solution.py
+++ b/solution.py
@@ -415,7 +415,7 @@
 
 def solution(mesh):
     groups, tp = mesh.shape["grp"], mesh.shape["tp"]
-    near = 4 if groups % 16 == 0 else 2
+    near = 8 if groups % 32 == 0 else 2
     ty = 4 if tp % 16 == 0 else 1
     torus = Mesh(
         mesh.devices.reshape(groups // (2 * near), near, 2, ty, tp // ty),

time: 135 us -> 147 us (1.089)
  blocking collectives: 92.5 us -> 105 us
    all_to_all x2, blocking collectives: 29.4 us -> 47.6 us  [on_device(): block = lax.all_to_all(block, NEAR, split_axis=0, concat_axis=0, tiled=True)]
    all_to_all x1, blocking collectives: 41.4 us -> 35.2 us  [on_device(): lax.all_to_all(block, 'far', split_axis=0, concat_axis=0, tiled=True)]
where the time goes in v7:
time: 147 us
  blocking collectives  105 us (71%)
  starting transfers between devices  30.4 us (21%)
  Pallas kernels  10.3 us (7%)
    all_to_all x2, blocking collectives, on_device(): block = lax.all_to_all(block, NEAR, split_axis=0, concat_axis=0, tiled=True)  47.6 us
    all_to_all x1, blocking collectives, on_device(): lax.all_to_all(block, 'far', split_axis=0, concat_axis=0, tiled=True)  35.2 us
    all_to_all x1, starting transfers between devices, on_device(): lax.all_to_all(flags.reshape(groups, 1, LANES), GRP, split_axis=0, concat...  30.4 us
    all_gather x2, blocking collectives, on_device(): stats = lax.all_gather(jnp.sum(lax.all_gather(stats, 'tx'), axis=0), 'ty')  21.9 us
    pallas_call x1, Pallas kernels, on_device(): pl.pallas_call(stats_kernel, out_shape=(jax.ShapeDtypeStruct((tokens, wid...  5.97 us
  transfers between devices with their start and end apart: 1, of which 0 were waited for; matrix products, arithmetic and copies ran while one was open for 0% of the time, Pallas kernels for 4%

profile of v7, /device:TPU:1, one launch (start us, length us, event | category | flops | bytes accessed | tf_op | source)
XLA Modules:
  0.0 146.9 jit_solution(2767710410819591371)
XLA Ops:
  1.3 1.6 %flags.1.after_ref = f32[64,128]{1,0:T(8,128)} custom-call(s32[1]{0:T(128)S(6)} %copy.15.length_ref, s32[1,384]{1,0:T(1,128)} %bitcast.20, s32[1,768]{1,0:T(1,128)} %rows_ref.3, f32[1,19]{1,0:T(1,128)} %targets_ref.1), custom_call_target="tpu_custom_call" | custom-call | tf_op jit(solution)/shard_map/flags/pallas_call | solution.py:341
  2.8 30.4 %all-to-all-start = ((f32[64,1,128]{2,1,0:T(1,128)}), f32[64,1,128]{2,1,0:T(1,128)S(1)}, u32[]{:S(2)}, u32[]{:S(2)}) async-start(f32[64,1,128]{2,1,0:T(1,128)} %bitcast.7), calls=%async_computation | async-start | bytes 65536 | tf_op jit(solution)/shard_map/all_to_all | solution.py:349
  33.2 0.0 copy-start
  33.3 0.0 copy-start.2
  33.3 0.0 copy-start.4
  33.3 6.0 %stats.1 = (bf16[384,512]{1,0:T(8,128)(2,1)S(1)}, f32[8,3584]{1,0:T(8,128)S(1)}) custom-call(f32[64,128]{1,0:T(8,128)} %flags.1.after_ref, bf16[384,5120]{1,0:T(8,128)(2,1)} %hidden_ref.1, bf16[5120,512]{1,0:T(8,128)(2,1)} %weight_ref.1, bf16[1024,512]{1,0:T(8,128)(2,1)} %text_ref.3, f32[1,512]{1,0:T(1,128)} %bitcast.24, f32[19,512]{1,0:T(8,128)} %bitcast.18), custom_call_target="tpu_custom_call" | custom-call | tf_op jit(solution)/shard_map/stats/pallas_call | solution.py:355
  39.3 0.0 copy-start.1
  39.3 0.0 copy-start.3
  39.3 0.0 copy-start.5
  39.3 11.3 %all-gather = f32[32,3584]{1,0:T(8,128)S(1)} all-gather(f32[8,3584]{1,0:T(8,128)S(1)} %get-tuple-element.12), channel_id=2, replica_groups=mesh['far'=4,'near'=8,'core'=2,'ty'=4,'tx'=4] {'tx'}, dimensions={0}, use_global_device_ids=true | all-gather | bytes 573440 | tf_op jit(solution)/shard_map/all_gather | solution.py:375
  50.6 10.6 %all-gather.1 = f32[32,3584]{1,0:T(8,128)S(1)} all-gather(f32[8,3584]{1,0:T(8,128)S(1)} %bitcast_reduce_fusion), channel_id=3, replica_groups=mesh['far'=4,'near'=8,'core'=2,'ty'=4,'tx'=4] {'ty'}, dimensions={0}, use_global_device_ids=true | all-gather | bytes 573440 | tf_op jit(solution)/shard_map/all_gather | solution.py:375
  61.2 0.0 all-to-all-done
  61.2 0.0 copy-done
  61.2 0.0 copy-done.4
  61.2 1.0 pooled.1
  62.2 28.1 %all_to_all.20.parts_ref = f32[16,4,640]{2,1,0:T(4,128)S(1)} all-to-all(f32[16,4,640]{2,1,0:T(4,128)S(1)} %reshape.37), channel_id=1, replica_groups=mesh['far'=4,'near'=8,'core'=2,'ty'=4,'tx'=4] {'near','core'}, dimensions={0} | all-to-all | bytes 327680 | tf_op jit(solution)/shard_map/all_to_all | solution.py:389
  90.3 0.1 fold_near.1
  90.4 35.2 %all_to_all.21.parts_ref = bf16[4,4,640]{2,1,0:T(4,128)(2,1)S(1)} all-to-all(bf16[4,4,640]{2,1,0:T(4,128)(2,1)S(1)} %fold_near.1), channel_id=1, replica_groups=mesh['far'=4,'near'=8,'core'=2,'ty'=4,'tx'=4] {'far'}, dimensions={0} | all-to-all | bytes 40960 | tf_op jit(solution)/shard_map/all_to_all | solution.py:391
  125.6 0.1 fold_far.1
  125.7 19.5 %all_to_all.22 = f32[16,4,640]{2,1,0:T(4,128)S(1)} all-to-all(f32[16,4,640]{2,1,0:T(4,128)S(1)} %fold_far.1), channel_id=1, replica_groups=mesh['far'=4,'near'=8,'core'=2,'ty'=4,'tx'=4] {'near','core'}, dimensions={0} | all-to-all | bytes 327680 | tf_op jit(solution)/shard_map/all_to_all | solution.py:393
  145.2 0.1 reshape.38.pooled_ref
  145.2 0.0 copy-done.1
  145.3 0.0 copy-done.3
  145.3 1.6 %grads.1 = (f32[1,128]{1,0:T(1,128)}, bf16[384,512]{1,0:T(8,128)(2,1)}, f32[19,512]{1,0:T(8,128)}, f32[1,512]{1,0:T(1,128)}) custom-call(s32[1]{0:T(128)} %bitcast.me_ref, f32[64,640]{1,0:T(8,128)S(1)} %reshape.38.pooled_ref, f32[24,384]{1,0:T(8,128)S(1)} %get-tuple-element.15.kept_ref, f32[64,128]{1,0:T(8,128)S(1)} %bitcast.17, s32[1,384]{1,0:T(1,128)S(1)} %bitcast.22, ...), custom_call_target="tpu_custom_call" | custom-call | tf_op jit(solution)/shard_map/grads/pallas_call | solution.py:396
  (4 shorter events, 0.1 us)
Async XLA Ops:
  2.8 58.4 %all-to-all-start = ((f32[64,1,128]{2,1,0:T(1,128)}), f32[64,1,128]{2,1,0:T(1,128)S(1)}, u32[]{:S(2)}, u32[]{:S(2)}) async-start(f32[64,1,128]{2,1,0:T(1,128)} %bitcast.7), calls=%async_computation | async-start | bytes 65536 | tf_op jit(solution)/shard_map/all_to_all | solution.py:349
  33.2 28.0 %copy-start = (bf16[1024,512]{1,0:T(8,128)(2,1)S(1)}, bf16[1024,512]{1,0:T(8,128)(2,1)}, u32[]{:S(2)}) copy-start(bf16[1024,512]{1,0:T(8,128)(2,1)} %text_ref.3) | copy-start | bytes 3145732
  33.3 27.9 %copy-start.2 = (s32[384,1]{0,1:T(1,128)S(1)}, s32[384,1]{0,1:T(1,128)}, u32[]{:S(2)}) copy-start(s32[384,1]{0,1:T(1,128)} %param.15) | copy-start | bytes 4612
  33.3 27.9 %copy-start.4 = (s32[1,768]{1,0:T(1,128)S(1)}, s32[1,768]{1,0:T(1,128)}, u32[]{:S(2)}) copy-start(s32[1,768]{1,0:T(1,128)} %rows_ref.3) | copy-start | bytes 9220
  39.3 106.0 %copy-start.1 = (f32[512,19]{0,1:T(8,128)S(1)}, f32[512,19]{0,1:T(8,128)}, u32[]{:S(2)}) copy-start(f32[512,19]{0,1:T(8,128)} %param.14) | copy-start | bytes 116740
  39.3 106.0 %copy-start.3 = (s32[64,19]{0,1:T(8,128)S(1)}, s32[64,19]{0,1:T(8,128)}, u32[]{:S(2)}) copy-start(s32[64,19]{0,1:T(8,128)} %param.18) | copy-start | bytes 14596
  39.3 106.0 %copy-start.5 = (f32[512]{0:T(512)S(1)}, f32[512]{0:T(512)}, u32[]{:S(2)}) copy-start(f32[512]{0:T(512)} %param.13) | copy-start | bytes 6148

commit v8 on v5

--- a/solution.py
+++ b/solution.py
@@ -81,7 +81,32 @@
     return jnp.concatenate([packed_stats[:, :rows], packed_stats[:, rows : 2 * rows], last], axis=0)
 
 
-def flags_kernel(cap, length_ref, owner_ref, rows_ref, targets_ref, out_ref):
+def fetched(sources, targets, arrived):
+    copies = []
+    for i, (source, target) in enumerate(zip(sources, targets)):
+        copies.append(pltpu.make_async_copy(source, target, arrived.at[i]))
+    for copy in copies:
+        copy.start()
+    return copies
+
+
+def flags_kernel(
+    cap,
+    length_ref,
+    owner_hbm,
+    rows_hbm,
+    targets_hbm,
+    out_ref,
+    owner_ref,
+    rows_ref,
+    targets_ref,
+    arrived,
+):
+    copies = fetched(
+        (owner_hbm, rows_hbm, targets_hbm), (owner_ref, rows_ref, targets_ref), arrived
+    )
+    for copy in copies:
+        copy.wait()
     groups = out_ref.shape[0]
     slots = rows_ref.shape[1]
     length = length_ref[0]
@@ -109,18 +134,22 @@
     hidden_ref,
     weight_ref,
     text_ref,
-    gain_ref,
-    head_ref,
+    gain_hbm,
+    head_hbm,
     visual_ref,
     stats_ref,
     hidden,
     weight,
     text,
     head,
+    gain_ref,
+    head_ref,
     arrived,
+    small_arrived,
 ):
     chunks, tokens, depth = hidden.shape
     objectives = head_ref.shape[0]
+    small = fetched((gain_hbm, head_hbm), (gain_ref, head_ref), small_arrived)
     copies = [pltpu.make_async_copy(text_ref, text, arrived.at[0])]
     for i in range(chunks):
         part = pl.ds(i * depth, depth)
@@ -132,6 +161,8 @@
         )
     for copy in copies:
         copy.start()
+    for copy in small:
+        copy.wait()
     gained = jnp.concatenate(in_three(gain_ref[...] * padded(head_ref, head)), axis=0)
 
     def of_rows(x):
@@ -341,8 +372,14 @@
     flags = pl.pallas_call(
         functools.partial(flags_kernel, cap),
         out_shape=jax.ShapeDtypeStruct((groups, LANES), jnp.float32),
-        in_specs=scalars(1) + whole(3),
+        in_specs=scalars(1) + [pl.BlockSpec(memory_space=pltpu.HBM)] * 3,
         out_specs=pl.BlockSpec(memory_space=pltpu.VMEM),
+        scratch_shapes=[
+            pltpu.VMEM(owners.shape, jnp.int32),
+            pltpu.VMEM(vis_row.shape, jnp.int32),
+            pltpu.VMEM(targets.shape, jnp.float32),
+            pltpu.SemaphoreType.DMA((3,)),
+        ],
         compiler_params=VMEM,
         name="flags",
     )(lengths, in_hbm(owners), in_hbm(vis_row), in_hbm(targets))
@@ -359,15 +396,17 @@
             jax.ShapeDtypeStruct((8, 2 * rows + tight_lanes(rows)), jnp.float32),
         ),
         in_specs=[pl.BlockSpec(memory_space=pl.ANY)]
-        + [pl.BlockSpec(memory_space=pltpu.HBM)] * 3
-        + whole(2),
+        + [pl.BlockSpec(memory_space=pltpu.HBM)] * 5,
         out_specs=tuple(whole(2)),
         scratch_shapes=[
             pltpu.VMEM((chunks, tokens, depth // chunks), jnp.bfloat16),
             pltpu.VMEM((chunks, depth // chunks, width), jnp.bfloat16),
             pltpu.VMEM((positions, width), jnp.bfloat16),
             pltpu.VMEM((K_ROWS, width), jnp.float32),
+            pltpu.VMEM(gain_row.shape, jnp.float32),
+            pltpu.VMEM(head.shape, jnp.float32),
             pltpu.SemaphoreType.DMA((2 * chunks + 1,)),
+            pltpu.SemaphoreType.DMA((2,)),
         ],
         compiler_params=VMEM,
         name="stats",

time: 135 us -> 136 us (level)
  transfers between devices with their start and end apart: 1 -> 1, of which waited for: 0 -> 0; matrix products, arithmetic and copies ran while one was open for 0% -> 0% of each run, Pallas kernels for 4% -> 5%
where the time goes in v8:
time: 136 us
  blocking collectives  92.6 us (68%)
  starting transfers between devices  30.4 us (22%)
  Pallas kernels  11.5 us (8%)
  between operations  1.39 us (1%)
    all_to_all x1, blocking collectives, on_device(): lax.all_to_all(block, 'far', split_axis=0, concat_axis=0, tiled=True)  41.4 us
    all_to_all x1, starting transfers between devices, on_device(): lax.all_to_all(flags.reshape(groups, 1, LANES), GRP, split_axis=0, concat...  30.4 us
    all_to_all x2, blocking collectives, on_device(): block = lax.all_to_all(block, NEAR, split_axis=0, concat_axis=0, tiled=True)  29.6 us
    all_gather x2, blocking collectives, on_device(): stats = lax.all_gather(jnp.sum(lax.all_gather(stats, 'tx'), axis=0), 'ty')  21.6 us
    pallas_call x1, Pallas kernels, on_device(): pl.pallas_call(stats_kernel, out_shape=(jax.ShapeDtypeStruct((tokens, wid...  7.18 us
  transfers between devices with their start and end apart: 1, of which 0 were waited for; matrix products, arithmetic and copies ran while one was open for 0% of the time, Pallas kernels for 5%

profile of v8, /device:TPU:1, one launch (start us, length us, event | category | flops | bytes accessed | tf_op | source)
XLA Modules:
  0.0 135.9 jit_solution(4523678369014605720)
XLA Ops:
  1.3 1.6 %flags.1.after_ref = f32[64,128]{1,0:T(8,128)} custom-call(s32[1]{0:T(128)S(6)} %copy.15.length_ref, s32[1,384]{1,0:T(1,128)} %bitcast.24, s32[1,768]{1,0:T(1,128)} %rows_ref.1, f32[1,19]{1,0:T(1,128)} %targets_hbm.1), custom_call_target="tpu_custom_call" | custom-call | tf_op jit(solution)/shard_map/flags/pallas_call | solution.py:372
  2.9 30.4 %all-to-all-start = ((f32[64,1,128]{2,1,0:T(1,128)}), f32[64,1,128]{2,1,0:T(1,128)S(1)}, u32[]{:S(2)}, u32[]{:S(2)}) async-start(f32[64,1,128]{2,1,0:T(1,128)} %bitcast.7), calls=%async_computation | async-start | bytes 65536 | tf_op jit(solution)/shard_map/all_to_all | solution.py:386
  33.3 0.0 copy-start
  33.3 0.0 copy-start.2
  33.3 0.0 copy-start.4
  33.3 0.0 copy-start.1
  33.3 0.0 copy-start.3
  33.4 0.0 copy-start.5
  33.4 7.2 %stats.1 = (bf16[384,512]{1,0:T(8,128)(2,1)S(1)}, f32[8,3584]{1,0:T(8,128)S(1)}) custom-call(f32[64,128]{1,0:T(8,128)} %flags.1.after_ref, bf16[384,5120]{1,0:T(8,128)(2,1)} %hidden_ref.1, bf16[5120,512]{1,0:T(8,128)(2,1)} %weight_ref.1, bf16[1024,512]{1,0:T(8,128)(2,1)} %text_ref.3, f32[1,512]{1,0:T(1,128)} %bitcast.28, f32[19,512]{1,0:T(8,128)} %bitcast.21), custom_call_target="tpu_custom_call" | custom-call | tf_op jit(solution)/shard_map/stats/pallas_call | solution.py:392
  40.6 11.2 %all-gather = f32[32,3584]{1,0:T(8,128)S(1)} all-gather(f32[8,3584]{1,0:T(8,128)S(1)} %get-tuple-element.12), channel_id=2, replica_groups=mesh['far'=8,'near'=4,'core'=2,'ty'=4,'tx'=4] {'tx'}, dimensions={0}, use_global_device_ids=true | all-gather | bytes 573440 | tf_op jit(solution)/shard_map/all_gather | solution.py:414
  51.7 10.4 %all-gather.1 = f32[32,3584]{1,0:T(8,128)S(1)} all-gather(f32[8,3584]{1,0:T(8,128)S(1)} %bitcast_reduce_fusion), channel_id=3, replica_groups=mesh['far'=8,'near'=4,'core'=2,'ty'=4,'tx'=4] {'ty'}, dimensions={0}, use_global_device_ids=true | all-gather | bytes 573440 | tf_op jit(solution)/shard_map/all_gather | solution.py:414
  62.2 0.0 all-to-all-done
  62.2 0.0 copy-done
  62.2 0.0 copy-done.2
  62.2 0.0 copy-done.4
  62.2 1.0 pooled.1
  63.2 16.1 %all_to_all.20.parts_ref = f32[8,8,640]{2,1,0:T(8,128)S(1)} all-to-all(f32[8,8,640]{2,1,0:T(8,128)S(1)} %bitcast.23), channel_id=1, replica_groups=mesh['far'=8,'near'=4,'core'=2,'ty'=4,'tx'=4] {'near','core'}, dimensions={0} | all-to-all | bytes 327680 | tf_op jit(solution)/shard_map/all_to_all | solution.py:428
  79.2 0.1 fold_near.1
  79.3 41.4 %all_to_all.21.parts_ref = bf16[8,8,640]{2,1,0:T(8,128)(2,1)S(1)} all-to-all(bf16[8,8,640]{2,1,0:T(8,128)(2,1)S(1)} %fold_near.1), channel_id=1, replica_groups=mesh['far'=8,'near'=4,'core'=2,'ty'=4,'tx'=4] {'far'}, dimensions={0} | all-to-all | bytes 163840 | tf_op jit(solution)/shard_map/all_to_all | solution.py:430
  120.7 0.1 fold_far.1
  120.8 13.5 %all_to_all.22 = f32[8,8,640]{2,1,0:T(8,128)S(1)} all-to-all(f32[8,8,640]{2,1,0:T(8,128)S(1)} %fold_far.1), channel_id=1, replica_groups=mesh['far'=8,'near'=4,'core'=2,'ty'=4,'tx'=4] {'near','core'}, dimensions={0} | all-to-all | bytes 327680 | tf_op jit(solution)/shard_map/all_to_all | solution.py:432
  134.3 0.0 copy-done.1
  134.3 0.0 copy-done.3
  134.3 1.6 %grads.1 = (f32[1,128]{1,0:T(1,128)}, bf16[384,512]{1,0:T(8,128)(2,1)}, f32[19,512]{1,0:T(8,128)}, f32[1,512]{1,0:T(1,128)}) custom-call(s32[1]{0:T(128)} %bitcast.me_ref, f32[64,640]{1,0:T(8,128)S(1)} %bitcast.18, f32[24,384]{1,0:T(8,128)S(1)} %get-tuple-element.15.kept_ref, f32[64,128]{1,0:T(8,128)S(1)} %bitcast.20, s32[1,384]{1,0:T(1,128)S(1)} %bitcast.26, ...), custom_call_target="tpu_custom_call" | custom-call | tf_op jit(solution)/shard_map/grads/pallas_call | solution.py:435
  (2 shorter events, 0.0 us)
Async XLA Ops:
  2.9 59.3 %all-to-all-start = ((f32[64,1,128]{2,1,0:T(1,128)}), f32[64,1,128]{2,1,0:T(1,128)S(1)}, u32[]{:S(2)}, u32[]{:S(2)}) async-start(f32[64,1,128]{2,1,0:T(1,128)} %bitcast.7), calls=%async_computation | async-start | bytes 65536 | tf_op jit(solution)/shard_map/all_to_all | solution.py:386
  33.3 28.9 %copy-start = (bf16[1024,512]{1,0:T(8,128)(2,1)S(1)}, bf16[1024,512]{1,0:T(8,128)(2,1)}, u32[]{:S(2)}) copy-start(bf16[1024,512]{1,0:T(8,128)(2,1)} %text_ref.3) | copy-start | bytes 3145732
  33.3 28.9 %copy-start.2 = (s32[384,1]{0,1:T(1,128)S(1)}, s32[384,1]{0,1:T(1,128)}, u32[]{:S(2)}) copy-start(s32[384,1]{0,1:T(1,128)} %param.15) | copy-start | bytes 4612
  33.3 28.9 %copy-start.4 = (s32[1,768]{1,0:T(1,128)S(1)}, s32[1,768]{1,0:T(1,128)}, u32[]{:S(2)}) copy-start(s32[1,768]{1,0:T(1,128)} %rows_ref.1) | copy-start | bytes 9220
  33.3 101.0 %copy-start.1 = (f32[512,19]{0,1:T(8,128)S(1)}, f32[512,19]{0,1:T(8,128)}, u32[]{:S(2)}) copy-start(f32[512,19]{0,1:T(8,128)} %param.14) | copy-start | bytes 116740
  33.3 101.0 %copy-start.3 = (s32[64,19]{0,1:T(8,128)S(1)}, s32[64,19]{0,1:T(8,128)}, u32[]{:S(2)}) copy-start(s32[64,19]{0,1:T(8,128)} %param.18) | copy-start | bytes 14596
  33.4 101.0 %copy-start.5 = (f32[512]{0:T(512)S(1)}, f32[512]{0:T(512)}, u32[]{:S(2)}) copy-start(f32[512]{0:T(512)} %param.13) | copy-start | bytes 6148

commit v9 on v5

--- a/solution.py
+++ b/solution.py
@@ -109,32 +109,39 @@
     hidden_ref,
     weight_ref,
     text_ref,
-    gain_ref,
-    head_ref,
+    gain_hbm,
+    head_hbm,
     visual_ref,
     stats_ref,
     hidden,
     weight,
     text,
     head,
+    gain_ref,
+    head_ref,
     arrived,
 ):
     chunks, tokens, depth = hidden.shape
     objectives = head_ref.shape[0]
-    copies = [pltpu.make_async_copy(text_ref, text, arrived.at[0])]
+    copies = []
     for i in range(chunks):
         part = pl.ds(i * depth, depth)
         copies.append(
-            pltpu.make_async_copy(hidden_ref.at[:, part], hidden.at[i], arrived.at[2 * i + 1])
+            pltpu.make_async_copy(hidden_ref.at[:, part], hidden.at[i], arrived.at[2 * i])
         )
         copies.append(
-            pltpu.make_async_copy(weight_ref.at[part, :], weight.at[i], arrived.at[2 * i + 2])
+            pltpu.make_async_copy(weight_ref.at[part, :], weight.at[i], arrived.at[2 * i + 1])
         )
-    for copy in copies:
+    late = 2 * chunks
+    others = [
+        pltpu.make_async_copy(gain_hbm, gain_ref, arrived.at[late]),
+        pltpu.make_async_copy(head_hbm, head_ref, arrived.at[late + 1]),
+        pltpu.make_async_copy(text_ref, text, arrived.at[late + 2]),
+    ]
+    for copy in copies[:4] + others + copies[4:]:
         copy.start()
-    gained = jnp.concatenate(in_three(gain_ref[...] * padded(head_ref, head)), axis=0)
-
-    def of_rows(x):
+
+    def of_rows(gained, x):
         parts = dot32(gained, x, LAST)
         value = parts[:K_ROWS] + parts[K_ROWS : 2 * K_ROWS] + parts[2 * K_ROWS :]
         wide = x.astype(jnp.float32)
@@ -146,17 +153,20 @@
         squares = dot32(jnp.ones((K_ROWS, terms.shape[1]), jnp.bfloat16), terms, LAST)
         return jnp.where(iota(value.shape, 0) == objectives, squares, value)
 
-    copies[0].wait()
-    of_text = of_rows(text[...])
     total = None
     for i in range(chunks):
+        copies[2 * i].wait()
         copies[2 * i + 1].wait()
-        copies[2 * i + 2].wait()
         part = dot32(hidden[i], weight[i], ALONG)
         total = part if total is None else total + part
+        if i == 1:
+            for copy in others:
+                copy.wait()
+            gained = jnp.concatenate(in_three(gain_ref[...] * padded(head_ref, head)), axis=0)
+            of_text = of_rows(gained, text[...])
     visual = total.astype(jnp.bfloat16)
     visual_ref[...] = visual
-    stats_ref[...] = tight(jnp.concatenate([of_rows(visual), of_text], axis=1))
+    stats_ref[...] = tight(jnp.concatenate([of_rows(gained, visual), of_text], axis=1))
 
 
 def pooled_kernel(
@@ -359,15 +369,16 @@
             jax.ShapeDtypeStruct((8, 2 * rows + tight_lanes(rows)), jnp.float32),
         ),
         in_specs=[pl.BlockSpec(memory_space=pl.ANY)]
-        + [pl.BlockSpec(memory_space=pltpu.HBM)] * 3
-        + whole(2),
+        + [pl.BlockSpec(memory_space=pltpu.HBM)] * 5,
         out_specs=tuple(whole(2)),
         scratch_shapes=[
             pltpu.VMEM((chunks, tokens, depth // chunks), jnp.bfloat16),
             pltpu.VMEM((chunks, depth // chunks, width), jnp.bfloat16),
             pltpu.VMEM((positions, width), jnp.bfloat16),
             pltpu.VMEM((K_ROWS, width), jnp.float32),
-            pltpu.SemaphoreType.DMA((2 * chunks + 1,)),
+            pltpu.VMEM(gain_row.shape, jnp.float32),
+            pltpu.VMEM(head.shape, jnp.float32),
+            pltpu.SemaphoreType.DMA((2 * chunks + 3,)),
         ],
         compiler_params=VMEM,
         name="stats",

time: 135 us -> 135 us (level)
  transfers between devices with their start and end apart: 1 -> 1, of which waited for: 0 -> 0; matrix products, arithmetic and copies ran while one was open for 0% -> 0% of each run, Pallas kernels for 4% -> 5%
where the time goes in v9:
time: 135 us
  blocking collectives  92.6 us (69%)
  starting transfers between devices  30.4 us (23%)
  Pallas kernels  10.3 us (8%)
  between operations  1.38 us (1%)
    all_to_all x1, blocking collectives, on_device(): lax.all_to_all(block, 'far', split_axis=0, concat_axis=0, tiled=True)  41.4 us
    all_to_all x1, starting transfers between devices, on_device(): lax.all_to_all(flags.reshape(groups, 1, LANES), GRP, split_axis=0, concat...  30.4 us
    all_to_all x2, blocking collectives, on_device(): block = lax.all_to_all(block, NEAR, split_axis=0, concat_axis=0, tiled=True)  29.5 us
    all_gather x2, blocking collectives, on_device(): stats = lax.all_gather(jnp.sum(lax.all_gather(stats, 'tx'), axis=0), 'ty')  21.7 us
    pallas_call x1, Pallas kernels, on_device(): pl.pallas_call(stats_kernel, out_shape=(jax.ShapeDtypeStruct((tokens, wid...  6.06 us
  transfers between devices with their start and end apart: 1, of which 0 were waited for; matrix products, arithmetic and copies ran while one was open for 0% of the time, Pallas kernels for 5%

profile of v9, /device:TPU:1, one launch (start us, length us, event | category | flops | bytes accessed | tf_op | source)
XLA Modules:
  0.0 134.7 jit_solution(15505893903365849154)
XLA Ops:
  1.3 1.6 %flags.1.after_ref = f32[64,128]{1,0:T(8,128)} custom-call(s32[1]{0:T(128)S(6)} %copy.15.length_ref, s32[1,384]{1,0:T(1,128)} %bitcast.24, s32[1,768]{1,0:T(1,128)} %rows_ref.3, f32[1,19]{1,0:T(1,128)} %targets_ref.1), custom_call_target="tpu_custom_call" | custom-call | tf_op jit(solution)/shard_map/flags/pallas_call | solution.py:351
  2.8 30.4 %all-to-all-start = ((f32[64,1,128]{2,1,0:T(1,128)}), f32[64,1,128]{2,1,0:T(1,128)S(1)}, u32[]{:S(2)}, u32[]{:S(2)}) async-start(f32[64,1,128]{2,1,0:T(1,128)} %bitcast.7), calls=%async_computation | async-start | bytes 65536 | tf_op jit(solution)/shard_map/all_to_all | solution.py:359
  33.2 0.0 copy-start
  33.3 0.0 copy-start.2
  33.3 0.0 copy-start.4
  33.3 0.0 copy-start.1
  33.3 0.0 copy-start.3
  33.3 0.0 copy-start.5
  33.3 6.1 %stats.1 = (bf16[384,512]{1,0:T(8,128)(2,1)S(1)}, f32[8,3584]{1,0:T(8,128)S(1)}) custom-call(f32[64,128]{1,0:T(8,128)} %flags.1.after_ref, bf16[384,5120]{1,0:T(8,128)(2,1)} %hidden_ref.1, bf16[5120,512]{1,0:T(8,128)(2,1)} %weight_ref.1, bf16[1024,512]{1,0:T(8,128)(2,1)} %text_ref.3, f32[1,512]{1,0:T(1,128)} %bitcast.28, f32[19,512]{1,0:T(8,128)} %bitcast.21), custom_call_target="tpu_custom_call" | custom-call | tf_op jit(solution)/shard_map/stats/pallas_call | solution.py:365
  39.4 11.2 %all-gather = f32[32,3584]{1,0:T(8,128)S(1)} all-gather(f32[8,3584]{1,0:T(8,128)S(1)} %get-tuple-element.12), channel_id=2, replica_groups=mesh['far'=8,'near'=4,'core'=2,'ty'=4,'tx'=4] {'tx'}, dimensions={0}, use_global_device_ids=true | all-gather | bytes 573440 | tf_op jit(solution)/shard_map/all_gather | solution.py:386
  50.6 10.6 %all-gather.1 = f32[32,3584]{1,0:T(8,128)S(1)} all-gather(f32[8,3584]{1,0:T(8,128)S(1)} %bitcast_reduce_fusion), channel_id=3, replica_groups=mesh['far'=8,'near'=4,'core'=2,'ty'=4,'tx'=4] {'ty'}, dimensions={0}, use_global_device_ids=true | all-gather | bytes 573440 | tf_op jit(solution)/shard_map/all_gather | solution.py:386
  61.2 0.0 all-to-all-done
  61.2 0.0 copy-done
  61.2 0.0 copy-done.2
  61.2 0.0 copy-done.4
  61.2 1.0 pooled.1
  62.1 15.9 %all_to_all.20.parts_ref = f32[8,8,640]{2,1,0:T(8,128)S(1)} all-to-all(f32[8,8,640]{2,1,0:T(8,128)S(1)} %bitcast.23), channel_id=1, replica_groups=mesh['far'=8,'near'=4,'core'=2,'ty'=4,'tx'=4] {'near','core'}, dimensions={0} | all-to-all | bytes 327680 | tf_op jit(solution)/shard_map/all_to_all | solution.py:400
  78.1 0.1 fold_near.1
  78.2 41.4 %all_to_all.21.parts_ref = bf16[8,8,640]{2,1,0:T(8,128)(2,1)S(1)} all-to-all(bf16[8,8,640]{2,1,0:T(8,128)(2,1)S(1)} %fold_near.1), channel_id=1, replica_groups=mesh['far'=8,'near'=4,'core'=2,'ty'=4,'tx'=4] {'far'}, dimensions={0} | all-to-all | bytes 163840 | tf_op jit(solution)/shard_map/all_to_all | solution.py:402
  119.5 0.1 fold_far.1
  119.6 13.5 %all_to_all.22 = f32[8,8,640]{2,1,0:T(8,128)S(1)} all-to-all(f32[8,8,640]{2,1,0:T(8,128)S(1)} %fold_far.1), channel_id=1, replica_groups=mesh['far'=8,'near'=4,'core'=2,'ty'=4,'tx'=4] {'near','core'}, dimensions={0} | all-to-all | bytes 327680 | tf_op jit(solution)/shard_map/all_to_all | solution.py:404
  133.1 0.0 copy-done.1
  133.1 0.0 copy-done.3
  133.2 1.6 %grads.1 = (f32[1,128]{1,0:T(1,128)}, bf16[384,512]{1,0:T(8,128)(2,1)}, f32[19,512]{1,0:T(8,128)}, f32[1,512]{1,0:T(1,128)}) custom-call(s32[1]{0:T(128)} %bitcast.me_ref, f32[64,640]{1,0:T(8,128)S(1)} %bitcast.18, f32[24,384]{1,0:T(8,128)S(1)} %get-tuple-element.15.kept_ref, f32[64,128]{1,0:T(8,128)S(1)} %bitcast.20, s32[1,384]{1,0:T(1,128)S(1)} %bitcast.26, ...), custom_call_target="tpu_custom_call" | custom-call | tf_op jit(solution)/shard_map/grads/pallas_call | solution.py:407
  (2 shorter events, 0.0 us)
Async XLA Ops:
  2.8 58.3 %all-to-all-start = ((f32[64,1,128]{2,1,0:T(1,128)}), f32[64,1,128]{2,1,0:T(1,128)S(1)}, u32[]{:S(2)}, u32[]{:S(2)}) async-start(f32[64,1,128]{2,1,0:T(1,128)} %bitcast.7), calls=%async_computation | async-start | bytes 65536 | tf_op jit(solution)/shard_map/all_to_all | solution.py:359
  33.2 27.9 %copy-start = (bf16[1024,512]{1,0:T(8,128)(2,1)S(1)}, bf16[1024,512]{1,0:T(8,128)(2,1)}, u32[]{:S(2)}) copy-start(bf16[1024,512]{1,0:T(8,128)(2,1)} %text_ref.3) | copy-start | bytes 3145732
  33.3 27.9 %copy-start.2 = (s32[384,1]{0,1:T(1,128)S(1)}, s32[384,1]{0,1:T(1,128)}, u32[]{:S(2)}) copy-start(s32[384,1]{0,1:T(1,128)} %param.15) | copy-start | bytes 4612
  33.3 27.9 %copy-start.4 = (s32[1,768]{1,0:T(1,128)S(1)}, s32[1,768]{1,0:T(1,128)}, u32[]{:S(2)}) copy-start(s32[1,768]{1,0:T(1,128)} %rows_ref.3) | copy-start | bytes 9220
  33.3 99.9 %copy-start.1 = (f32[512,19]{0,1:T(8,128)S(1)}, f32[512,19]{0,1:T(8,128)}, u32[]{:S(2)}) copy-start(f32[512,19]{0,1:T(8,128)} %param.14) | copy-start | bytes 116740
  33.3 99.9 %copy-start.3 = (s32[64,19]{0,1:T(8,128)S(1)}, s32[64,19]{0,1:T(8,128)}, u32[]{:S(2)}) copy-start(s32[64,19]{0,1:T(8,128)} %param.18) | copy-start | bytes 14596
  33.3 99.8 %copy-start.5 = (f32[512]{0:T(512)S(1)}, f32[512]{0:T(512)}, u32[]{:S(2)}) copy-start(f32[512]{0:T(512)} %param.13) | copy-start | bytes 6148
